TPU v7x, 256 devices: a whole 4x4x8 slice. The times are simulated.
256 devices in a mesh: seq: 32 (over x, y, core), tp: 8 (over z).
Axes of the slice: x: 4, y: 4, z: 8, core: 2. Of those that a mesh axis runs over, the one named last changes fastest.
Arguments:
- hidden: bfloat16 [40960, 8192], P('seq', 'tp'), may hold values from -6 to 6
- queries: bfloat16 [40960, 8192], P('seq', 'tp'), may hold values from -8 to 8
- keys_values: bfloat16 [2, 40960, 1024], P(None, 'seq', 'tp'), may hold values from -8 to 8
- w_router: bfloat16 [8192], P('tp'), may hold values from -0.0625 to 0.0625
- routed: int32 [32, 160], P('seq'), may hold values from 0 to 1279, as said below
- counts: int32 [32], replicated, may hold values from 1 to 160, 3200 in all
- grad_out: bfloat16 [5120, 8192], P('seq', 'tp'), may hold values from -6 to 6
Outputs:
- branch_out: bfloat16 [5120, 8192], P('seq', 'tp')
- grad_queries: bfloat16 [5120, 8192], P('seq', 'tp')
- grad_keys_values: bfloat16 [2, 5120, 1024], P(None, 'seq', 'tp')
- grad_router: float32 [8192], P('tp')
Inputs may be any that keep to these rules, and one draw needn't show every extreme that they name: Each row lists 160 different positions of one shard's tokens in increasing order; the first counts entries of a row are the shard's routed tokens. `counts`: each shard has at least one live slot and one shard has all 160.
All inputs are finite; a program needn't handle non-finite values.
Results may differ from a plain program's by a relative error of at most 0.03.
Values may be sent and summed in bfloat16 or wider, within the bound.
A program may use at most 128 MiB of HBM per device.

v0:
```python
import math

import jax
import jax.numpy as jnp
from jax import lax
from jax.sharding import PartitionSpec as P

HEAD_WIDTH = 128


def copy_for_each(array, axis):
    copies = jnp.broadcast_to(array, (lax.axis_size(axis), *array.shape))
    return lax.all_to_all(copies, axis, split_axis=0, concat_axis=0, tiled=True)


def taken_together(array, axis):
    everything = copy_for_each(array, axis)
    return jnp.sum(everything, axis=0)


def shards(hidden, queries, keys_values, w_router, routed, counts, grad_out):
    seq_count = lax.axis_size("seq")
    own_shard = lax.axis_index("seq")
    capacity = routed.shape[1]
    kv_local = keys_values.shape[2] // HEAD_WIDTH
    q_local = queries.shape[1] // HEAD_WIDTH
    group = q_local // kv_local
    logit_scale_factor = 1.0 / math.sqrt(HEAD_WIDTH)
    chosen_slots = routed[0]
    live_rows = (jnp.arange(capacity, dtype=jnp.int32) < counts[own_shard]).astype(jnp.float32)
    key_live = (jnp.arange(capacity, dtype=jnp.int32)[None, :] < counts[:, None]).reshape(-1)
    query_slots = own_shard * capacity + jnp.arange(capacity, dtype=jnp.int32)
    last_slot = own_shard * capacity + capacity - 1
    chosen_x = hidden[chosen_slots]
    logit = lax.psum(jnp.dot(chosen_x, w_router, preferred_element_type=jnp.float32), "tp")
    gate = jax.nn.sigmoid(logit)
    weight_rows = gate * live_rows
    routed_query_rows = queries[chosen_slots].reshape(capacity, kv_local, group, HEAD_WIDTH)
    own_pairs = keys_values[:, chosen_slots]
    per_block = min(max(1, -(-512 // capacity)), seq_count)
    while seq_count % per_block:
        per_block += 1
    block_rows = per_block * capacity
    block_total = seq_count // per_block

    def score_block(key_block, first_row):
        row_count = key_block.shape[1]
        routed_key_rows = key_block[0].reshape(row_count, kv_local, HEAD_WIDTH)
        routed_value_rows = key_block[1].reshape(row_count, kv_local, HEAD_WIDTH)
        score_matrix = (
            jnp.einsum(
                "vemc,uec->emvu",
                routed_query_rows,
                routed_key_rows,
                preferred_element_type=jnp.float32,
            )
            * logit_scale_factor
        )
        key_slots = first_row + jnp.arange(row_count, dtype=jnp.int32)
        allowed = (key_slots[None, :] <= query_slots[:, None]) & lax.dynamic_slice_in_dim(
            key_live, first_row, row_count
        )[None, :]
        return (score_matrix, allowed, routed_key_rows, routed_value_rows)

    def forward_block(carried, key_block, first_row):

        def forward_work(held):
            running_max, running_sum, accumulated = held
            score_matrix, allowed, routed_key_rows, routed_value_rows = score_block(
                key_block, first_row
            )
            block_max = jnp.max(jnp.where(allowed, score_matrix, -1e30), axis=-1)
            new_max = jnp.maximum(running_max, block_max)
            exponentials = jnp.where(allowed, jnp.exp(score_matrix - new_max[..., None]), 0.0)
            factor = jnp.exp(running_max - new_max)
            running_sum = running_sum * factor + jnp.sum(exponentials, axis=-1)
            accumulated = accumulated * factor[..., None] + jnp.einsum(
                "eujh,hey->eujy",
                exponentials.astype(jnp.bfloat16),
                routed_value_rows,
                preferred_element_type=jnp.float32,
            )
            return (new_max, running_sum, accumulated)

        return lax.cond(first_row <= last_slot, forward_work, lambda held: held, carried)

    start_state = (
        jnp.full((kv_local, group, capacity), -1e30, jnp.float32),
        jnp.zeros((kv_local, group, capacity), jnp.float32),
        jnp.zeros((kv_local, group, capacity, HEAD_WIDTH), jnp.float32),
    )
    gathered = lax.all_gather(own_pairs, "seq", axis=1, tiled=True)

    def forward_step(index_block, carried):
        first_row = index_block * block_rows
        return forward_block(
            carried, lax.dynamic_slice_in_dim(gathered, first_row, block_rows, 1), first_row
        )

    running_max, running_sum, accumulated = lax.fori_loop(0, block_total, forward_step, start_state)
    lse = running_max + jnp.log(running_sum)
    attention_output = (accumulated / running_sum[..., None]).transpose(2, 0, 1, 3)
    branch_out = (
        (attention_output * weight_rows[:, None, None, None])
        .reshape(capacity, q_local * HEAD_WIDTH)
        .astype(jnp.bfloat16)
    )
    upstream = grad_out.astype(jnp.float32).reshape(capacity, kv_local, group, HEAD_WIDTH)
    gradient_rows = (upstream * weight_rows[:, None, None, None]).astype(jnp.bfloat16)
    gate_term = lax.psum(jnp.sum(upstream * attention_output, axis=(1, 2, 3)), "tp")
    dlogit = gate_term * gate * (1.0 - gate) * live_rows
    grad_router = taken_together(jnp.dot(dlogit, chosen_x.astype(jnp.float32)), "seq")
    delta = jnp.sum(gradient_rows.astype(jnp.float32) * attention_output, axis=-1).transpose(
        1, 2, 0
    )

    def backward_terms(key_block, first_row):
        score_matrix, allowed, routed_key_rows, routed_value_rows = score_block(
            key_block, first_row
        )
        probs = jnp.where(allowed, jnp.exp(score_matrix - lse[..., None]), 0.0)
        probs_narrow = probs.astype(jnp.bfloat16)
        prob_gradient = jnp.einsum(
            "vemc,uec->emvu", gradient_rows, routed_value_rows, preferred_element_type=jnp.float32
        )
        score_gradient = (probs * (prob_gradient - delta[..., None])).astype(jnp.bfloat16)
        return (score_gradient, probs_narrow, routed_key_rows)

    def key_value_terms(score_gradient, probs_narrow):
        key_gradient = (
            jnp.einsum(
                "cfym,ycfh->mch",
                score_gradient,
                routed_query_rows,
                preferred_element_type=jnp.float32,
            )
            * logit_scale_factor
        )
        value_gradient = jnp.einsum(
            "cfym,ycfh->mch", probs_narrow, gradient_rows, preferred_element_type=jnp.float32
        )
        return (
            key_gradient.reshape(capacity * lax.axis_size("seq"), kv_local * HEAD_WIDTH),
            value_gradient.reshape(capacity * lax.axis_size("seq"), kv_local * HEAD_WIDTH),
        )

    def query_step(index_block, query_acc):
        first_row = index_block * block_rows
        key_block = lax.dynamic_slice_in_dim(gathered, first_row, block_rows, 1)

        def query_work(held):
            score_gradient, probs_narrow, routed_key_rows = backward_terms(key_block, first_row)
            return held + jnp.einsum(
                "psot,tpn->opsn",
                score_gradient,
                routed_key_rows,
                preferred_element_type=jnp.float32,
            )

        return lax.cond(first_row <= last_slot, query_work, lambda held: held, query_acc)

    query_acc = lax.fori_loop(
        0, block_total, query_step, jnp.zeros((capacity, kv_local, group, HEAD_WIDTH), jnp.float32)
    )
    start = jnp.int32(0)
    key_block = gathered

    def destination_work(unused):
        score_gradient, probs_narrow, routed_key_rows = backward_terms(key_block, start)
        key_gradient, value_gradient = key_value_terms(score_gradient, probs_narrow)
        return jnp.stack([key_gradient, value_gradient], axis=1)

    summed = lax.psum_scatter(
        lax.cond(
            start <= last_slot,
            destination_work,
            lambda unused: jnp.zeros(
                (capacity * lax.axis_size("seq"), 2, kv_local * HEAD_WIDTH), jnp.float32
            ),
            0,
        ).astype(jnp.bfloat16),
        "seq",
        scatter_dimension=0,
        tiled=True,
    ).astype(jnp.float32)
    grad_keys_values = summed.transpose(1, 0, 2).astype(jnp.bfloat16)
    grad_queries = (
        (query_acc * logit_scale_factor)
        .reshape(capacity, q_local * HEAD_WIDTH)
        .astype(jnp.bfloat16)
    )
    return (branch_out, grad_queries, grad_keys_values, grad_router)


def solution(mesh):
    in_specs = (
        P("seq", "tp"),
        P("seq", "tp"),
        P(None, "seq", "tp"),
        P("tp"),
        P("seq", None),
        P(),
        P("seq", "tp"),
    )
    out_specs = (P("seq", "tp"), P("seq", "tp"), P(None, "seq", "tp"), P("tp"))
    return jax.shard_map(shards, mesh=mesh, in_specs=in_specs, out_specs=out_specs, check_vma=False)
```

profile of v0, /device:TPU:24, one launch (start us, length us, event | category | flops | bytes accessed | tf_op | source)
XLA Modules:
  0.0 278.6 jit_solution(15035105167879202028)
XLA Ops:
  8.1 6.0 %gather_fusion = bf16[160,2,128]{2,0,1:T(8,128)(2,1)} fusion(bf16[2,1280,128]{2,1,0:T(8,128)(2,1)} %param.19, s32[1024]{0:T(1024)S(1)} %pad_clamp_fusion), kind=kCustom, calls=%fused_computation | custom fusion | bytes 164480 | tf_op jit(solution)/shard_map/gather | solution.py:39
  16.5 3.3 %gather_fusion.1 = bf16[160,1024]{1,0:T(8,128)(2,1)S(1)} fusion(bf16[1280,1024]{1,0:T(8,128)(2,1)} %param.18, s32[1024]{0:T(1024)S(1)} %pad_clamp_fusion), kind=kCustom, calls=%fused_computation.1 | custom fusion | bytes 656000 | tf_op jit(solution)/shard_map/gather | solution.py:38
  23.7 20.0 %psum.14 = f32[160]{0:T(256)S(1)} all-reduce(f32[160]{0:T(256)S(1)} %bitcast.288), channel_id=1, replica_groups=mesh['seq'=32,'tp'=8] {'tp'}, use_global_device_ids=true, to_apply=%region_6.7 | all-reduce | flops 160 | bytes 1280 | tf_op jit(solution)/shard_map/psum | solution.py:35
  46.4 19.7 %all-gather.3.cloned.1.call-done = bf16[2,5120,128]{2,1,0:T(8,128)(2,1)} async-done(((bf16[2,160,128]{2,1,0:T(8,128)(2,1)}), bf16[2,5120,128]{2,1,0:T(8,128)(2,1)}) %all-gather.3.cloned.1.call-update) | async-done | bytes 2621456 | tf_op jit(solution)/shard_map/all_gather | solution.py:92
  67.0 13.2 %while.35 = (s32[]{:T(128)}, f32[1,8,160]{2,1,0:T(8,128)S(1)}, f32[1,8,160]{2,1,0:T(8,128)S(1)}, f32[1,8,160,128]{3,2,1,0:T(8,128)}, s32[]{:T(128)}, /*index=5*/...) while((s32[]{:T(128)}, f32[1,8,160]{2,1,0:T(8,128)S(1)}, ...), condition=%wide.region_5.6_spmd.clone, body=%wide.region_0.5_spmd.clone.sunk | while | flops 428983840 | bytes 12354389 | solution.py:100
  67.0 6.3 %conditional.8 = ((f32[1,8,160]{2,1,0:T(8,128)S(1)}, f32[1,8,160]{2,1,0:T(8,128)S(1)}, f32[1,8,160,128]{3,2,1,0:T(8,128)})) conditional(s32[]{:T(128)} %convert_element_type.132, (f32[1,8,160]{2,1,0:T(8,128)S(1)}, f32[1,8,160]{2,1,0:T(8,128)S(1)}, f32[1,8,160,128]{3,2,1,0:T(8,128)}) %tuple.123, (s32[]{:T(128)}, s32[]{:T(128)}, ...), branch_computations={%region_1.1_spmd, %region_2.4_spmd} | conditional | flops 428983840 | bytes 12333030 | solution.py:85
  69.4 2.9 %fusion.20 = f32[1,8,160,128]{3,2,1,0:T(8,128)} fusion(f32[640,160,8]{0,1,2:T(8,128)S(1)} %get-tuple-element.794, f32[8,160]{1,0:T(8,128)S(1)} %bitcast.270, pred[160,640]{1,0:T(8,128)(4,1)S(1)} %compare_and_fusion, f32[1,8,160,128]{3,2,1,0:T(8,128)} %get-tuple-element.494, f32[8,160]{1,0:T(8,128)S(1)} %get-tuple-element.791, ...), kind=kOutput, calls=%fused_computation.18 | convolution fusion | flops 213319680 | bytes 4864008 | tf_op jit(solution)/shard_map/while/body/eval_jaxpr/cond/branch_1_fun/eujh,hey->eujy/dot_general | solution.py:77
  73.4 6.3 %conditional.8 = ((f32[1,8,160]{2,1,0:T(8,128)S(1)}, f32[1,8,160]{2,1,0:T(8,128)S(1)}, f32[1,8,160,128]{3,2,1,0:T(8,128)})) conditional(s32[]{:T(128)} %convert_element_type.132, (f32[1,8,160]{2,1,0:T(8,128)S(1)}, f32[1,8,160]{2,1,0:T(8,128)S(1)}, f32[1,8,160,128]{3,2,1,0:T(8,128)}) %tuple.123, (s32[]{:T(128)}, s32[]{:T(128)}, ...), branch_computations={%region_1.1_spmd, %region_2.4_spmd} | conditional | flops 428983840 | bytes 12333030 | solution.py:85
  75.8 2.9 %fusion.20 = f32[1,8,160,128]{3,2,1,0:T(8,128)} fusion(f32[640,160,8]{0,1,2:T(8,128)S(1)} %get-tuple-element.794, f32[8,160]{1,0:T(8,128)S(1)} %bitcast.270, pred[160,640]{1,0:T(8,128)(4,1)S(1)} %compare_and_fusion, f32[1,8,160,128]{3,2,1,0:T(8,128)} %get-tuple-element.494, f32[8,160]{1,0:T(8,128)S(1)} %get-tuple-element.791, ...), kind=kOutput, calls=%fused_computation.18 | convolution fusion | flops 213319680 | bytes 4864008 | tf_op jit(solution)/shard_map/while/body/eval_jaxpr/cond/branch_1_fun/eujh,hey->eujy/dot_general | solution.py:77
  80.3 4.4 %fusion.101 = (f32[160]{0:T(256)S(1)}, f32[160,8]{1,0:T(8,128)S(1)}, bf16[160,1,8,128]{3,2,0,1:T(8,128)(2,1)}) fusion(f32[20,8,8,128]{3,2,1,0:T(8,128)} %copy.58, f32[8,160]{0,1:T(8,128)S(1)} %copy.45, f32[1,8,160,128]{3,2,1,0:T(8,128)} %get-tuple-element.544, bf16[160,1,8,128]{3,2,0,1:T(8,128)(2,1)} %fusion.100, f32[160]{0:T(256)S(1)} %fusion.104), kind=kLoop, calls=%fused_computation.101 | loop fusion | flops 1309280 | bytes 1977600 | tf_op jit(solution)/shard_map/reduce_sum | solution.py:110
  84.7 48.1 %conditional.3 = (bf16[5120,2,128]{2,0,1:T(8,128)(2,1)}) conditional(s32[]{:T(128)} %convert_element_type.88, () %tuple.73, (s32[]{:T(128)}, s32[32]{0:T(128)S(1)}, s32[32,160]{1,0:T(8,128)S(1)}, bf16[2,5120,128]{2,1,0:T(8,128)(2,1)}, bf16[160,1,8,128]{3,2,0,1:T(8,128)(2,1)S(1)}, /*index=5*/f32[1,8,160]{2,1,0:T(8,128)S(1)}, ...), branch_computations={%region_12.0_spmd, %region_13.0_spmd} | conditional | flops 6780687360 | bytes 98208800 | solution.py:174
  86.5 11.9 %fusion.81 = f32[5120,160,8]{0,1,2:T(8,128)} fusion(bf16[2,5120,128]{2,1,0:T(8,128)(2,1)} %get-tuple-element.531, bf16[160,1,8,128]{3,2,0,1:T(8,128)(2,1)S(1)} %get-tuple-element.730), kind=kOutput, calls=%fused_computation.80 | convolution fusion | flops 1677721600 | bytes 27852800 | tf_op jit(solution)/shard_map/cond/branch_1_fun/vemc,uec->emvu/dot_general | solution.py:51
  98.4 20.5 %fusion.75 = bf16[5120,1,128]{2,0,1:T(8,128)(2,1)} fusion(f32[5120,160,8]{0,1,2:T(8,128)} %fusion.81, f32[8,160]{1,0:T(8,128)S(1)} %bitcast.286, f32[8,160]{1,0:T(8,128)S(1)} %bitcast.282, pred[160,5120]{1,0:T(8,128)(4,1)} %fusion.78, bf16[2,5120,128]{2,1,0:T(8,128)(2,1)} %get-tuple-element.531, bf16[160,1,8,128]{3,2,0,1:T(8,128)(2,1)} %get-tuple-element.732, ...), kind=kOutput, calls=%fused_computation.75 | convolution fusion | flops 3396075520 | bytes 30320640 | tf_op jit(solution)/shard_map/cond/branch_1_fun/cfym,ycfh->mch/dot_general | solution.py:131
  118.9 12.2 %fusion.69 = bf16[5120,1,128]{2,0,1:T(8,128)(2,1)S(1)} fusion(f32[5120,160,8]{0,1,2:T(8,128)} %fusion.81, f32[8,160]{1,0:T(8,128)S(1)} %bitcast.283, pred[160,5120]{1,0:T(8,128)(4,1)} %fusion.78, bf16[160,1,8,128]{3,2,0,1:T(8,128)(2,1)} %get-tuple-element.732), kind=kOutput, calls=%fused_computation.73 | convolution fusion | flops 1703936000 | bytes 28677120 | tf_op jit(solution)/shard_map/cond/branch_1_fun/cfym,ycfh->mch/dot_general | solution.py:139
  134.9 16.6 %while.36 = (s32[]{:T(128)}, f32[160,1,8,128]{3,0,2,1:T(8,128)}, s32[]{:T(128)}, bf16[2,5120,128]{2,1,0:T(8,128)(2,1)}, bf16[160,1,8,128]{3,0,2,1:T(8,128)(2,1)S...) while((s32[]{:T(128)}, f32[160,1,8,128]{3,0,2,1:T(8,128)}, ...), condition=%wide.region_11.12_spmd.clone, body=%wide.region_8.11_spmd.clone.sunk | while | flops 634435328 | bytes 9293617 | solution.py:162
  134.9 8.1 %conditional.9 = (f32[160,1,8,128]{3,0,2,1:T(8,128)}) conditional(s32[]{:T(128)} %convert_element_type.133, f32[160,1,8,128]{3,0,2,1:T(8,128)} %get-tuple-element.972, (s32[]{:T(128)}, bf16[2,5120,128]{2,1,0:T(8,128)(2,1)}, s32[]{:T(128)}, s32[32,160]{1,0:T(8,128)S(1)}, bf16[160,1,8,128]{3,0,2,1:T(8,128)(2,1)S(1)}, ...), branch_computations={%region_9.9_spmd, %region_10.10_spmd} | conditional | flops 634435328 | bytes 9272266 | solution.py:160
  135.3 3.2 %fusion.42 = f32[640,160,8]{0,1,2:T(8,128)} fusion(bf16[160,1,8,128]{3,0,2,1:T(8,128)(2,1)S(1)} %get-tuple-element.515, bf16[2,5120,128]{2,1,0:T(8,128)(2,1)} %get-tuple-element.509, s32[]{:T(128)S(6)} %add.169, s32[]{:T(128)S(6)} %select_n.59), kind=kOutput, calls=%fused_computation.46 | convolution fusion | flops 209715200 | bytes 3768328 | tf_op jit(solution)/shard_map/while/body/eval_jaxpr/cond/branch_1_fun/vemc,uec->emvu/dot_general | solution.py:123
  138.5 4.5 %fusion.39 = f32[160,1,8,128]{3,0,2,1:T(8,128)} fusion(f32[160,1,8,128]{3,0,2,1:T(8,128)} %get-tuple-element.508, f32[8,160]{1,0:T(8,128)S(1)} %bitcast.285, f32[640,160,8]{0,1,2:T(8,128)} %fusion.42, f32[8,160]{1,0:T(8,128)S(1)} %bitcast.284, pred[160,640]{1,0:T(8,128)(4,1)S(1)} %compare_and_fusion.1, bf16[160,1,8,128]{3,0,2,1:T(8,128)(2,1)S(1)} %get-tuple-element.513, ...), kind=kOutput, calls=%fused_computation.44 | convolution fusion | flops 424509440 | bytes 5356544 | tf_op jit(solution)/shard_map/while/body/eval_jaxpr/cond/branch_1_fun/psot,tpn->opsn/dot_general | solution.py:153
  143.0 8.1 %conditional.9 = (f32[160,1,8,128]{3,0,2,1:T(8,128)}) conditional(s32[]{:T(128)} %convert_element_type.133, f32[160,1,8,128]{3,0,2,1:T(8,128)} %get-tuple-element.972, (s32[]{:T(128)}, bf16[2,5120,128]{2,1,0:T(8,128)(2,1)}, s32[]{:T(128)}, s32[32,160]{1,0:T(8,128)S(1)}, bf16[160,1,8,128]{3,0,2,1:T(8,128)(2,1)S(1)}, ...), branch_computations={%region_9.9_spmd, %region_10.10_spmd} | conditional | flops 634435328 | bytes 9272266 | solution.py:160
  143.4 3.2 %fusion.42 = f32[640,160,8]{0,1,2:T(8,128)} fusion(bf16[160,1,8,128]{3,0,2,1:T(8,128)(2,1)S(1)} %get-tuple-element.515, bf16[2,5120,128]{2,1,0:T(8,128)(2,1)} %get-tuple-element.509, s32[]{:T(128)S(6)} %add.169, s32[]{:T(128)S(6)} %select_n.59), kind=kOutput, calls=%fused_computation.46 | convolution fusion | flops 209715200 | bytes 3768328 | tf_op jit(solution)/shard_map/while/body/eval_jaxpr/cond/branch_1_fun/vemc,uec->emvu/dot_general | solution.py:123
  146.6 4.5 %fusion.39 = f32[160,1,8,128]{3,0,2,1:T(8,128)} fusion(f32[160,1,8,128]{3,0,2,1:T(8,128)} %get-tuple-element.508, f32[8,160]{1,0:T(8,128)S(1)} %bitcast.285, f32[640,160,8]{0,1,2:T(8,128)} %fusion.42, f32[8,160]{1,0:T(8,128)S(1)} %bitcast.284, pred[160,640]{1,0:T(8,128)(4,1)S(1)} %compare_and_fusion.1, bf16[160,1,8,128]{3,0,2,1:T(8,128)(2,1)S(1)} %get-tuple-element.513, ...), kind=kOutput, calls=%fused_computation.44 | convolution fusion | flops 424509440 | bytes 5356544 | tf_op jit(solution)/shard_map/while/body/eval_jaxpr/cond/branch_1_fun/psot,tpn->opsn/dot_general | solution.py:153
  152.8 17.5 %psum.15 = f32[160]{0:T(256)S(1)} all-reduce(f32[160]{0:T(256)S(1)} %get-tuple-element.751), channel_id=1, replica_groups=mesh['seq'=32,'tp'=8] {'tp'}, use_global_device_ids=true, to_apply=%region_16.17 | all-reduce | flops 160 | bytes 1280 | tf_op jit(solution)/shard_map/psum | solution.py:110
  172.7 92.3 %all-to-all-start = ((f32[32,1,1024]{2,1,0:T(1,128)}), f32[32,1,1024]{2,1,0:T(1,128)S(1)}, u32[]{:S(2)}, u32[]{:S(2)}) async-start(f32[32,1,1024]{2,1,0:T(1,128)} %broadcast_in_dim.77), calls=%async_computation.1 | async-start | bytes 262144 | tf_op jit(solution)/shard_map/all_to_all | solution.py:13
  266.9 4.1 %all-to-all-done = f32[32,1,1024]{2,1,0:T(1,128)S(1)} async-done(((f32[32,1,1024]{2,1,0:T(1,128)}), f32[32,1,1024]{2,1,0:T(1,128)S(1)}, u32[]{:S(2)}, u32[]{:S(2)}) %all-to-all-start) | async-done | bytes 131104 | tf_op jit(solution)/shard_map/all_to_all | solution.py:13
  (124 shorter events, 30.6 us)
Async XLA Ops:
  7.2 7.7 %copy-start = (bf16[1280,1024]{1,0:T(8,128)(2,1)S(1)}, bf16[1280,1024]{1,0:T(8,128)(2,1)}, u32[]{:S(2)}) copy-start(bf16[1280,1024]{1,0:T(8,128)(2,1)} %param.17) | copy-start | bytes 7864324
  7.2 58.9 %all-gather.3.cloned.1.call-start = ((), (), s32[]{:S(2)}) async-start(), calls=%async_computation.3 | async-start | bytes 2703360 | tf_op jit(solution)/shard_map/all_gather | solution.py:92
  14.1 257.7 %reduce-scatter.2.cloned.1.call-start = ((), (), s32[]{:S(2)}) async-start(), calls=%async_computation.2 | async-start | bytes 2703360 | tf_op jit(solution)/shard_map/reduce_scatter | solution.py:173
  16.5 5.4 %copy-start.2 = (s32[32]{0:T(128)S(1)}, s32[32]{0:T(128)}, u32[]{:S(2)}) copy-start(s32[32]{0:T(128)} %param.22) | copy-start | bytes 388
  118.9 12.2 %copy-start.1 = (bf16[5120,1,128]{2,0,1:T(8,128)(2,1)S(1)}, bf16[5120,1,128]{2,0,1:T(8,128)(2,1)}, u32[]{:S(2)}) copy-start(bf16[5120,1,128]{2,0,1:T(8,128)(2,1)} %fusion.75) | copy-start | bytes 3932164 | tf_op jit(solution)/shard_map/cond
  172.7 98.4 %all-to-all-start = ((f32[32,1,1024]{2,1,0:T(1,128)}), f32[32,1,1024]{2,1,0:T(1,128)S(1)}, u32[]{:S(2)}, u32[]{:S(2)}) async-start(f32[32,1,1024]{2,1,0:T(1,128)} %broadcast_in_dim.77), calls=%async_computation.1 | async-start | bytes 262144 | tf_op jit(solution)/shard_map/all_to_all | solution.py:13
Sparse Core Ops, SparseCore 0:
  14.2 51.8 all-gather.2
  133.0 124.1 reduce-scatter.1
where the time goes:
time: 283 us; the launch traced here: 279 us
  starting transfers between devices  92.4 us (33%)
  matrix products  71.8 us (25%)
  blocking collectives  37.5 us (13%)
  waiting for transfers between devices  23.9 us (8%)
  local copies, waits for them, and re-layouts  20.2 us (7%)
  other arithmetic  17.7 us (6%)
  between operations  14.2 us (5%)
    all_to_all x1, starting transfers between devices, copy_for_each(): return lax.all_to_all(copies, axis, split_axis=0, concat_axis=0, tiled=True)  92.3 us
    dot_general x1, matrix products, key_value_terms(): jnp.einsum('cfym,ycfh->mch', score_gradient, routed_query_rows, preferred...  20.5 us
    psum x1, blocking collectives, shards(): lax.psum(jnp.dot(chosen_x, w_router, preferred_element_type=jnp.float32),...  20 us
    all_gather x1, waiting for transfers between devices, shards(): gathered = lax.all_gather(own_pairs, 'seq', axis=1, tiled=True)  19.7 us
    psum x1, blocking collectives, shards(): lax.psum(jnp.sum(upstream * attention_output, axis=(1, 2, 3)), 'tp')  17.5 us
    dot_general x3, matrix products, score_block(): jnp.einsum('vemc,uec->emvu', routed_query_rows, routed_key_rows, preferre...  15.7 us
    dot_general x1, matrix products, key_value_terms(): jnp.einsum('cfym,ycfh->mch', probs_narrow, gradient_rows, preferred_eleme...  12.2 us
    dot_general x2, matrix products, query_work(): jnp.einsum('psot,tpn->opsn', score_gradient, routed_key_rows, preferred_e...  8.92 us
  transfers between devices with their start and end apart: 3, of which 2 were waited for; matrix products, arithmetic and copies ran while one was open for 13% of the time, Pallas kernels for 0%

commit v1 on v0

v1 whole, which is shorter than its diff:
```python
import functools
import math

import jax
import jax.numpy as jnp
from jax import lax
from jax.experimental import pallas as pl
from jax.experimental.pallas import tpu as pltpu
from jax.sharding import PartitionSpec as P

HEAD_WIDTH = 128
MESH = pl.DeviceIdType.MESH
NEG = -1e30
CHUNK = 256
LIVE_SHARE = (5, 8)
F32 = jnp.float32
BF16 = jnp.bfloat16


def dot_nn(a, b):
    return lax.dot_general(a, b, (((1,), (0,)), ((), ())), preferred_element_type=F32)


def dot_nt(a, b):
    return lax.dot_general(a, b, (((1,), (1,)), ((), ())), preferred_element_type=F32)


def dot_tn(a, b):
    return lax.dot_general(a, b, (((0,), (0,)), ((), ())), preferred_element_type=F32)


def rows_of(row, cap):
    return jnp.broadcast_to(row, (128, cap)).T


def fetch_kernel(nseq, ntp, hid, qry, kv, w, routed, x_out, q_out, kvall, logit_out,
                 hid_v, qry_v, kv_v, part, lsem, ssem, rsem, fsem, gsem, tssem, trsem):
    me, mt = lax.axis_index("seq"), lax.axis_index("tp")
    nchip = nseq // 2
    chip, core = me // 2, me % 2
    sib = me + 1 - 2 * core
    cap = routed.shape[1]
    tok = hid.shape[0]
    heads = q_out.shape[0]
    load_kv = pltpu.make_async_copy(kv, kv_v, lsem.at[0])
    load_hid = pltpu.make_async_copy(hid, hid_v, lsem.at[1])
    load_qry = pltpu.make_async_copy(qry, qry_v, lsem.at[2])
    load_kv.start()
    load_hid.start()
    load_qry.start()

    barrier = pltpu.get_barrier_semaphore()

    def greet_chip(c, _):
        @pl.when(c < chip)
        def _():
            pl.semaphore_signal(barrier, inc=1, device_id={"seq": 2 * c + core}, device_id_type=MESH)
        return 0

    def greet_tp(t, _):
        @pl.when(t != mt)
        def _():
            pl.semaphore_signal(barrier, inc=1, device_id={"tp": t}, device_id_type=MESH)
        return 0

    lax.fori_loop(0, nchip, greet_chip, 0)
    pl.semaphore_signal(barrier, inc=1, device_id={"seq": sib}, device_id_type=MESH)
    lax.fori_loop(0, ntp, greet_tp, 0)

    col = rows_of(routed[...].astype(F32), cap)
    lane = lax.broadcasted_iota(jnp.int32, (cap, 128), 1).astype(F32)
    onehot = jnp.concatenate(
        [jnp.where(col == lane + 128.0 * j, 1.0, 0.0).astype(BF16) for j in range(tok // 128)], axis=1
    )
    load_kv.wait()
    kvall[me, :, 0:128] = dot_nn(onehot, kv_v[0]).astype(BF16)
    kvall[me, :, 128:256] = dot_nn(onehot, kv_v[1]).astype(BF16)

    pl.semaphore_wait(barrier, nchip - 1 - chip + 1 + ntp - 1)

    def to_chip(c):
        return pltpu.make_async_remote_copy(
            src_ref=kvall.at[me], dst_ref=kvall.at[me], send_sem=ssem.at[c], recv_sem=rsem.at[chip],
            device_id={"seq": 2 * c + core}, device_id_type=MESH)

    def send_chip(i, _):
        c = nchip - 1 - i

        @pl.when(c > chip)
        def _():
            to_chip(c).start()
        return 0

    def own_to_sib():
        return pltpu.make_async_remote_copy(
            src_ref=kvall.at[me], dst_ref=kvall.at[me], send_sem=fsem.at[chip], recv_sem=gsem.at[chip],
            device_id={"seq": sib}, device_id_type=MESH)

    lax.fori_loop(0, nchip, send_chip, 0)

    @pl.when(core == 0)
    def _():
        own_to_sib().start()

    load_hid.wait()
    x = dot_nn(onehot, hid_v[...]).astype(BF16)
    x_out[...] = x
    logit = dot_nt(jnp.broadcast_to(w[...], (16, w.shape[1])), x)
    part[mt, :, :] = jnp.zeros((8, 256), F32)
    part[mt, :, 0:cap] = logit[0:8]

    def to_tp(t):
        return pltpu.make_async_remote_copy(
            src_ref=part.at[mt], dst_ref=part.at[mt], send_sem=tssem.at[t], recv_sem=trsem.at[mt],
            device_id={"tp": t}, device_id_type=MESH)

    def from_tp(t):
        return pltpu.make_async_remote_copy(
            src_ref=part.at[t], dst_ref=part.at[t], send_sem=tssem.at[t], recv_sem=trsem.at[t],
            device_id={"tp": t}, device_id_type=MESH)

    def send_tp(t, _):
        @pl.when(t != mt)
        def _():
            to_tp(t).start()
        return 0

    lax.fori_loop(0, ntp, send_tp, 0)

    load_qry.wait()
    for h in range(heads):
        q_out[h] = dot_nn(onehot, qry_v[:, h * 128:(h + 1) * 128]).astype(BF16)

    def wait_tp(t, _):
        @pl.when(t != mt)
        def _():
            from_tp(t).wait_recv()
        return 0

    lax.fori_loop(0, ntp, wait_tp, 0)
    total = part[0]
    for t in range(1, ntp):
        total = total + part[t]
    logit_out[...] = total

    def landed(c):
        block = kvall.at[2 * c + core]
        return pltpu.make_async_remote_copy(
            src_ref=block, dst_ref=block, send_sem=fsem.at[c], recv_sem=rsem.at[c],
            device_id={"seq": sib}, device_id_type=MESH)

    def forward(c):
        block = kvall.at[2 * c + core]
        return pltpu.make_async_remote_copy(
            src_ref=block, dst_ref=block, send_sem=fsem.at[c], recv_sem=gsem.at[c],
            device_id={"seq": sib}, device_id_type=MESH)

    def forwarded(c):
        block = kvall.at[2 * c + 1 - core]
        return pltpu.make_async_remote_copy(
            src_ref=block, dst_ref=block, send_sem=fsem.at[c], recv_sem=gsem.at[c],
            device_id={"seq": sib}, device_id_type=MESH)

    def pass_on(i, _):
        c = chip - 1 - i

        @pl.when(c >= 0)
        def _():
            landed(c).wait_recv()
            forward(c).start()
        return 0

    lax.fori_loop(0, nchip, pass_on, 0)

    def finish(c, _):
        @pl.when(c < chip)
        def _():
            forwarded(c).wait_recv()
            forward(c).wait_send()

        @pl.when(c > chip)
        def _():
            to_chip(c).wait_send()
        return 0

    lax.fori_loop(0, nchip, finish, 0)

    @pl.when(core == 0)
    def _():
        own_to_sib().wait_send()

    @pl.when(core == 1)
    def _():
        forwarded(chip).wait_recv()

    def finish_tp(t, _):
        @pl.when(t != mt)
        def _():
            to_tp(t).wait_send()
        return 0

    lax.fori_loop(0, ntp, finish_tp, 0)


def attend_kernel(scale, counts, kvall, q, g, logit, branch, dq, contrib, own, gterm,
                  kx, vx, qtx, dotx, dob, s_scr, e_scr, ot, wide, dkv):
    me = lax.axis_index("seq")
    cap, width = g.shape
    nq = q.shape[0]
    heads = width // 128
    to_exp2 = scale * math.log2(math.e)
    live_here = counts[me]

    row = lax.broadcasted_iota(jnp.int32, (cap, 128), 0)
    lane = lax.broadcasted_iota(jnp.int32, (cap, 128), 1)
    ones3 = jnp.where(lane < 3, 1.0, 0.0).astype(BF16)
    kx[0:cap, 0:128] = kvall[me, :, 0:128]
    kx[0:cap, 128:256] = jnp.zeros((cap, 128), BF16)
    vx[0:cap, 0:128] = kvall[me, :, 128:256]
    vx[0:cap, 128:256] = ones3

    def place(s, off):
        off = pl.multiple_of(off, 16)
        n = counts[s]
        kx[pl.ds(off, cap), 0:128] = kvall[s, :, 0:128]
        kx[pl.ds(off, cap), 128:256] = jnp.where((row >= n) & (lane == 0), NEG, 0.0).astype(BF16)
        vx[pl.ds(off, cap), 0:128] = kvall[s, :, 128:256]
        vx[pl.ds(off, cap), 128:256] = ones3
        return off + ((n + 15) // 16) * 16

    end = pl.multiple_of(lax.fori_loop(0, me, place, cap), 16)
    kx[pl.ds(end, CHUNK), 0:128] = jnp.zeros((CHUNK, 128), BF16)
    kx[pl.ds(end, CHUNK), 128:256] = jnp.where(
        lax.broadcasted_iota(jnp.int32, (CHUNK, 128), 1) == 0, NEG, 0.0).astype(BF16)
    vx[pl.ds(end, CHUNK), :] = jnp.zeros((CHUNK, 256), BF16)
    chunks = (end - cap + CHUNK - 1) // CHUNK

    def at(c):
        return pl.ds(pl.multiple_of(cap + c * CHUNK, 32), CHUNK)

    qtx[0:128, :] = q[...].T
    first = lax.broadcasted_iota(jnp.int32, (128, nq), 0)
    qtx[128:256, :] = jnp.where(first == 0, 1.0, 0.0).astype(BF16)

    key_slot = lax.broadcasted_iota(jnp.int32, (cap, nq), 0)
    pos = lax.broadcasted_iota(jnp.int32, (cap, nq), 1)
    query_slot = pos
    for h in range(1, heads):
        query_slot = query_slot - jnp.where(pos >= h * cap, cap, 0)
    s = jnp.where(key_slot <= query_slot, dot_nn(kx[0:cap, :], qtx[...]), NEG)
    s_scr[0:cap, :] = s
    top = jnp.max(s.reshape(cap // 8, 8, nq), axis=0)

    def score(c, top):
        s = dot_nn(kx[at(c), :], qtx[...])
        s_scr[at(c), :] = s
        return jnp.maximum(top, jnp.max(s.reshape(CHUNK // 8, 8, nq), axis=0))

    top = lax.fori_loop(0, chunks, score, top)
    top = jnp.max(top, axis=0, keepdims=True) * to_exp2

    def soften(sl, rows, total, start):
        e = jnp.exp2(s_scr[sl, :] * to_exp2 - top)
        eb = e.astype(BF16)
        e_scr[sl, :] = eb
        add = dot_tn(vx[sl, 0:128], eb)
        ot[...] = add if start else ot[...] + add
        return total + jnp.sum(e.reshape(rows // 8, 8, nq), axis=0)

    total = soften(pl.ds(0, cap), cap, jnp.zeros((8, nq), F32), True)
    total = lax.fori_loop(0, chunks, lambda c, t: soften(at(c), CHUNK, t, False), total)
    inverse = 1.0 / jnp.sum(total, axis=0, keepdims=True)

    z = logit[0:1, 0:cap]
    gate = 1.0 / (1.0 + jnp.exp(-z))
    live = lax.broadcasted_iota(jnp.int32, (1, cap), 1) < live_here
    weight = rows_of(jnp.where(live, gate, 0.0), cap)
    factor = jnp.where(live, gate * (1.0 - gate), 0.0)
    ot[...] = ot[...] * inverse
    wide[...] = ot[...].T
    acc = jnp.zeros((cap, 128), F32)
    for h in range(heads):
        rows, lanes = slice(h * cap, (h + 1) * cap), slice(h * 128, (h + 1) * 128)
        o = wide[rows, :]
        up = g[:, lanes].astype(F32)
        branch[:, lanes] = (o * weight).astype(BF16)
        acc = acc + up * o
        wide[rows, :] = up * weight
    gterm[0:8, :] = jnp.zeros((8, 256), F32)
    gterm[0:1, 0:cap] = jnp.sum(acc.T, axis=0, keepdims=True)
    gterm[1:2, 0:cap] = factor
    cot = (wide[...].T * inverse).astype(BF16)
    dotx[0:128, :] = cot
    cotf = cot.astype(F32)
    delta = -jnp.sum(cotf * ot[...], axis=0, keepdims=True)
    d1 = delta.astype(BF16).astype(F32)
    d2 = (delta - d1).astype(BF16).astype(F32)
    d3 = delta - d1 - d2
    dotx[128:256, :] = jnp.where(
        first == 0, d1, jnp.where(first == 1, d2, jnp.where(first == 2, d3, 0.0))).astype(BF16)
    dob[...] = cotf.T.astype(BF16)

    def back(sl, start):
        e = e_scr[sl, :]
        ds = (e.astype(F32) * dot_nn(vx[sl, :], dotx[...])).astype(BF16)
        add = dot_tn(kx[sl, 0:128], ds)
        wide_t = ot
        wide_t[...] = add if start else wide_t[...] + add
        return dot_nn(ds, q[...]) * scale, dot_nn(e, dob[...])

    dk, dv = back(pl.ds(0, cap), True)
    own[:, 0:128] = dk
    own[:, 128:256] = dv

    def back_chunk(c, _):
        dk, dv = back(at(c), False)
        dkv[at(c), 0:128] = dk.astype(BF16)
        dkv[at(c), 128:256] = dv.astype(BF16)
        return 0

    lax.fori_loop(0, chunks, back_chunk, 0)

    wide[...] = (ot[...] * scale).T
    for h in range(heads):
        dq[:, h * 128:(h + 1) * 128] = wide[h * cap:(h + 1) * cap, :].astype(BF16)

    row2 = lax.broadcasted_iota(jnp.int32, (cap, 256), 0)

    def unplace(s, off):
        off = pl.multiple_of(off, 16)
        n = counts[s]
        block = dkv[pl.ds(off, cap), :].astype(F32)
        contrib[s % 2, s // 2] = jnp.where(row2 < n, block, 0.0).astype(BF16)
        return off + ((n + 15) // 16) * 16

    lax.fori_loop(0, me, unplace, cap)


def return_kernel(nseq, ntp, contrib, own, gterm, x, dkv_out, router_out,
                  pair, mine, inbox, part, gpair, gchip, sums, psem, prsem, ssem, rsem, tssem, trsem,
                  qsem, qrsem, gssem, grsem):
    me, mt = lax.axis_index("seq"), lax.axis_index("tp")
    nchip = nseq // 2
    chip, core = me // 2, me % 2
    sib = me + 1 - 2 * core
    cap = x.shape[0]

    barrier = pltpu.get_barrier_semaphore()

    def greet_chip(c, _):
        @pl.when(c != chip)
        def _():
            pl.semaphore_signal(barrier, inc=1, device_id={"seq": 2 * c + core}, device_id_type=MESH)
        return 0

    def greet_tp(t, _):
        @pl.when(t != mt)
        def _():
            pl.semaphore_signal(barrier, inc=1, device_id={"tp": t}, device_id_type=MESH)
        return 0

    lax.fori_loop(0, nchip, greet_chip, 0)
    pl.semaphore_signal(barrier, inc=1, device_id={"seq": sib}, device_id_type=MESH)
    lax.fori_loop(0, ntp, greet_tp, 0)
    part[mt] = gterm[...]
    pl.semaphore_wait(barrier, nchip - 1 + 1 + ntp - 1)

    def tp_copy(slot, t):
        return pltpu.make_async_remote_copy(
            src_ref=part.at[slot], dst_ref=part.at[slot], send_sem=tssem.at[t], recv_sem=trsem.at[slot],
            device_id={"tp": t}, device_id_type=MESH)

    def send_tp(t, _):
        @pl.when(t != mt)
        def _():
            tp_copy(mt, t).start()
        return 0

    lax.fori_loop(0, ntp, send_tp, 0)

    def pair_copy(c):
        return pltpu.make_async_remote_copy(
            src_ref=contrib.at[1 - core, c], dst_ref=pair.at[c], send_sem=psem.at[c], recv_sem=prsem.at[c],
            device_id={"seq": sib}, device_id_type=MESH)

    def send_pair(c, _):
        @pl.when((c < chip) | ((c == chip) & (core == 1)))
        def _():
            pair_copy(c).start()
        return 0

    lax.fori_loop(0, nchip, send_pair, 0)

    def chip_copy(c):
        return pltpu.make_async_remote_copy(
            src_ref=mine.at[c], dst_ref=inbox.at[chip], send_sem=ssem.at[c], recv_sem=rsem.at[chip],
            device_id={"seq": 2 * c + core}, device_id_type=MESH)

    def join(c, _):
        @pl.when(c < chip)
        def _():
            pair_copy(c).wait_recv()
            mine[c] = (contrib[core, c].astype(F32) + pair[c].astype(F32)).astype(BF16)
            chip_copy(c).start()
        return 0

    lax.fori_loop(0, nchip, join, 0)

    def wait_tp(t, _):
        @pl.when(t != mt)
        def _():
            tp_copy(t, t).wait_recv()
        return 0

    lax.fori_loop(0, ntp, wait_tp, 0)
    total = part[0, 0:1, :]
    for t in range(1, ntp):
        total = total + part[t, 0:1, :]
    dlogit = (total * gterm[1:2, :])[:, 0:cap]
    p1 = dlogit.astype(BF16)
    r1 = dlogit - p1.astype(F32)
    p2 = r1.astype(BF16)
    p3 = (r1 - p2.astype(F32)).astype(BF16)
    xs = x[...]
    share = (dot_nn(jnp.broadcast_to(p1, (16, cap)), xs) + dot_nn(jnp.broadcast_to(p2, (16, cap)), xs)
             + dot_nn(jnp.broadcast_to(p3, (16, cap)), xs))
    for i in range(8):
        gpair[core, i:i + 1, :] = share[0:1, i * 128:(i + 1) * 128]

    def gpair_copy(slot):
        return pltpu.make_async_remote_copy(
            src_ref=gpair.at[slot], dst_ref=gpair.at[slot], send_sem=qsem, recv_sem=qrsem,
            device_id={"seq": sib}, device_id_type=MESH)

    gpair_copy(core).start()
    gpair_copy(1 - core).wait_recv()
    gchip[chip] = gpair[0] + gpair[1]

    def gchip_copy(slot, c):
        return pltpu.make_async_remote_copy(
            src_ref=gchip.at[slot], dst_ref=gchip.at[slot], send_sem=gssem.at[c], recv_sem=grsem.at[slot],
            device_id={"seq": 2 * c + core}, device_id_type=MESH)

    def send_gchip(c, _):
        @pl.when(c != chip)
        def _():
            gchip_copy(chip, c).start()
        return 0

    lax.fori_loop(0, nchip, send_gchip, 0)

    @pl.when(core == 0)
    def _():
        pair_copy(chip).wait_recv()
        pair[nchip] = pair[chip]

    @pl.when(core == 1)
    def _():
        pair[nchip] = jnp.zeros((cap, 256), BF16)

    def inbox_copy(c):
        return pltpu.make_async_remote_copy(
            src_ref=inbox.at[c], dst_ref=inbox.at[c], send_sem=ssem.at[c], recv_sem=rsem.at[c],
            device_id={"seq": 2 * c + core}, device_id_type=MESH)

    sums[...] = own[...] + pair[nchip].astype(F32)

    def add(c, _):
        @pl.when(c > chip)
        def _():
            inbox_copy(c).wait_recv()
            sums[...] = sums[...] + inbox[c].astype(F32)
        return 0

    lax.fori_loop(0, nchip, add, 0)
    dkv_out[0] = sums[:, 0:128].astype(BF16)
    dkv_out[1] = sums[:, 128:256].astype(BF16)

    def wait_gchip(c, _):
        @pl.when(c != chip)
        def _():
            gchip_copy(c, c).wait_recv()
        return 0

    lax.fori_loop(0, nchip, wait_gchip, 0)
    total = gchip[0]
    for c in range(1, nchip):
        total = total + gchip[c]
    router_out[...] = total

    gpair_copy(core).wait_send()

    def finish(c, _):
        @pl.when((c < chip) | ((c == chip) & (core == 1)))
        def _():
            pair_copy(c).wait_send()

        @pl.when(c < chip)
        def _():
            chip_copy(c).wait_send()

        @pl.when(c != chip)
        def _():
            gchip_copy(chip, c).wait_send()
        return 0

    lax.fori_loop(0, nchip, finish, 0)

    def finish_tp(t, _):
        @pl.when(t != mt)
        def _():
            tp_copy(mt, t).wait_send()
        return 0

    lax.fori_loop(0, ntp, finish_tp, 0)


def vmem(n=1):
    specs = [pl.BlockSpec(memory_space=pltpu.VMEM) for _ in range(n)]
    return specs if n > 1 else specs[0]


def shards(hidden, queries, keys_values, w_router, routed, counts, grad_out):
    nseq, ntp = lax.axis_size("seq"), lax.axis_size("tp")
    nchip = nseq // 2
    cap = routed.shape[1]
    tok, width = queries.shape
    heads = width // HEAD_WIDTH
    nq = heads * cap
    scale = 1.0 / math.sqrt(HEAD_WIDTH)
    dma, shape = pltpu.SemaphoreType.DMA, jax.ShapeDtypeStruct
    anywhere = pl.BlockSpec(memory_space=pl.ANY)

    x, q, kvall, logit = pl.pallas_call(
        functools.partial(fetch_kernel, nseq, ntp),
        out_shape=(shape((cap, width), BF16), shape((heads, cap, 128), BF16),
                   shape((nseq, cap, 256), BF16), shape((8, 256), F32)),
        in_specs=[anywhere] * 3 + vmem(2),
        out_specs=tuple(vmem(4)),
        scratch_shapes=[
            pltpu.VMEM((tok, width), BF16), pltpu.VMEM((tok, width), BF16), pltpu.VMEM((2, tok, 128), BF16),
            pltpu.VMEM((ntp, 8, 256), F32), dma((3,)), dma((nchip,)), dma((nchip,)), dma((nchip,)),
            dma((nchip,)), dma((ntp,)), dma((ntp,)),
        ],
        compiler_params=pltpu.CompilerParams(
            collective_id=0, has_side_effects=True, vmem_limit_bytes=40 * 2 ** 20),
        name="fetch",
    )(hidden, queries, keys_values, w_router.reshape(1, width), routed)

    live = nseq * cap * LIVE_SHARE[0] // LIVE_SHARE[1]
    span = -(-(live + 15 * nseq) // CHUNK) * CHUNK
    rows = cap + span + CHUNK
    branch, dq, contrib, own, gterm = pl.pallas_call(
        functools.partial(attend_kernel, scale),
        out_shape=(shape((cap, width), BF16), shape((cap, width), BF16),
                   shape((2, nchip, cap, 256), BF16), shape((cap, 256), F32), shape((8, 256), F32)),
        in_specs=[pl.BlockSpec(memory_space=pltpu.SMEM)] + vmem(4),
        out_specs=tuple(vmem(5)),
        scratch_shapes=[
            pltpu.VMEM((rows, 256), BF16), pltpu.VMEM((rows, 256), BF16),
            pltpu.VMEM((256, nq), BF16), pltpu.VMEM((256, nq), BF16), pltpu.VMEM((nq, 128), BF16),
            pltpu.VMEM((cap + span, nq), F32), pltpu.VMEM((cap + span, nq), BF16),
            pltpu.VMEM((128, nq), F32), pltpu.VMEM((nq, 128), F32), pltpu.VMEM((rows, 256), BF16),
        ],
        compiler_params=pltpu.CompilerParams(vmem_limit_bytes=60 * 2 ** 20),
        name="attend",
    )(counts, kvall, q.reshape(nq, 128), grad_out, logit)

    dkv, router = pl.pallas_call(
        functools.partial(return_kernel, nseq, ntp),
        out_shape=(shape((2, cap, 128), BF16), shape((8, 128), F32)),
        in_specs=vmem(4),
        out_specs=tuple(vmem(2)),
        scratch_shapes=[
            pltpu.VMEM((nchip + 1, cap, 256), BF16), pltpu.VMEM((nchip, cap, 256), BF16),
            pltpu.VMEM((nchip, cap, 256), BF16), pltpu.VMEM((ntp, 8, 256), F32),
            pltpu.VMEM((2, 8, 128), F32), pltpu.VMEM((nchip, 8, 128), F32), pltpu.VMEM((cap, 256), F32),
            dma((nchip,)), dma((nchip,)), dma((nchip,)), dma((nchip,)), dma((ntp,)), dma((ntp,)),
            dma, dma, dma((nchip,)), dma((nchip,)),
        ],
        compiler_params=pltpu.CompilerParams(
            collective_id=1, has_side_effects=True, vmem_limit_bytes=40 * 2 ** 20),
        name="settle",
    )(contrib, own, gterm, x)
    return branch, dq, dkv, router.reshape(8 * 128)


def solution(mesh):
    in_specs = (
        P("seq", "tp"),
        P("seq", "tp"),
        P(None, "seq", "tp"),
        P("tp"),
        P("seq", None),
        P(),
        P("seq", "tp"),
    )
    out_specs = (P("seq", "tp"), P("seq", "tp"), P(None, "seq", "tp"), P("tp"))
    return jax.shard_map(shards, mesh=mesh, in_specs=in_specs, out_specs=out_specs, check_vma=False)
```

time: 283 us -> 98.1 us (0.35); the launches traced: 279 us -> 97.7 us
  starting transfers between devices: 92.4 us -> 0 us
  Pallas kernels: 0 us -> 83.7 us
  matrix products: 71.8 us -> 0 us
  blocking collectives: 37.5 us -> 0 us
  waiting for transfers between devices: 23.9 us -> 0 us
  other arithmetic: 17.7 us -> 0 us
  between operations: 14.2 us -> 0.67 us
  local copies, waits for them, and re-layouts: 20.2 us -> 13.4 us
    all_to_all x1 -> x0, starting transfers between devices: 92.3 us -> none  [copy_for_each(): return lax.all_to_all(copies, axis, split_axis=0, concat_axis=0, tiled=True)]
    pallas_call x0 -> x3, Pallas kernels: none -> 83.7 us  [the longest x1 51.4 us: shards(): pl.pallas_call(functools.partial(return_kernel, nseq, ntp), out_shape=(sh...]
    dot_general x13 -> x0, matrix products: 71.8 us -> none  [the longest x1 20.5 us: key_value_terms(): jnp.einsum('cfym,ycfh->mch', score_gradient, routed_query_rows, preferred...]
    psum x2 -> x0, blocking collectives: 37.5 us -> none  [the longest x1 20 us: shards(): lax.psum(jnp.dot(chosen_x, w_router, preferred_element_type=jnp.float32),...]
    all_gather x1 -> x0, waiting for transfers between devices: 19.7 us -> none  [shards(): gathered = lax.all_gather(own_pairs, 'seq', axis=1, tiled=True)]
    gather x3 -> x0, local copies, waits for them, and re-layouts: 11 us -> none  [the longest x1 6.03 us: shards(): own_pairs = keys_values[:, chosen_slots]]
    unnamed x10 -> x22, local copies, waits for them, and re-layouts: 2.85 us -> 12.7 us
    reduce_sum x4 -> x0, other arithmetic: 7.13 us -> none  [the longest x1 4.39 us: shards(): jnp.sum(upstream * attention_output, axis=(1, 2, 3))]
  transfers between devices with their start and end apart: 3 -> 0, of which waited for: 2 -> 0; matrix products, arithmetic and copies ran while one was open for 13% -> 0% of each run, Pallas kernels for 0% -> 0%
where the time goes in v1:
time: 98.1 us; the launch traced here: 97.7 us
  Pallas kernels  83.7 us (85%)
  local copies, waits for them, and re-layouts  13.4 us (14%)
    pallas_call x1, Pallas kernels, shards(): pl.pallas_call(functools.partial(return_kernel, nseq, ntp), out_shape=(sh...  51.4 us
    pallas_call x1, Pallas kernels, shards(): pl.pallas_call(functools.partial(fetch_kernel, nseq, ntp), out_shape=(sha...  23 us
    unnamed x22, local copies, waits for them, and re-layouts  12.7 us
    pallas_call x1, Pallas kernels, shards(): pl.pallas_call(functools.partial(attend_kernel, scale), out_shape=(shape(...  9.31 us

profile of v1, /device:TPU:24, one launch (start us, length us, event | category | flops | bytes accessed | tf_op | source)
XLA Modules:
  0.0 97.7 jit_solution(2708084404402165379)
XLA Ops:
  0.6 0.7 reshape.17.w
  1.3 0.0 copy-start
  1.3 1.7 %copy-done = bf16[1280,1024]{1,0:T(8,128)(2,1)S(1)} copy-done((bf16[1280,1024]{1,0:T(8,128)(2,1)S(1)}, bf16[1280,1024]{1,0:T(8,128)(2,1)}, u32[]{:S(2)}) %copy-start) | copy-done | bytes 2621464
  3.1 0.0 copy-start.1
  3.1 1.7 %copy-done.1 = bf16[1280,1024]{1,0:T(8,128)(2,1)S(1)} copy-done((bf16[1280,1024]{1,0:T(8,128)(2,1)S(1)}, bf16[1280,1024]{1,0:T(8,128)(2,1)}, u32[]{:S(2)}) %copy-start.1) | copy-done | bytes 2621464
  4.8 0.0 copy-start.4
  4.8 1.1 %copy-done.4 = bf16[2,1280,128]{2,1,0:T(8,128)(2,1)S(1)} copy-done((bf16[2,1280,128]{2,1,0:T(8,128)(2,1)S(1)}, bf16[2,1280,128]{2,1,0:T(8,128)(2,1)}, u32[]{:S(2)}) %copy-start.4) | copy-done | bytes 655384
  5.9 0.0 copy-start.9
  5.9 0.7 copy-done.9
  6.6 23.0 %fetch.1 = (bf16[160,1024]{1,0:T(8,128)(2,1)S(1)}, bf16[8,160,128]{2,1,0:T(8,128)(2,1)S(1)}, bf16[32,160,256]{2,1,0:T(8,128)(2,1)S(1)}, f32[8,256]{1,0:T(8,128)S(1)}) custom-call(bf16[1280,1024]{1,0:T(8,128)(2,1)S(1)} %copy-done, bf16[1280,1024]{1,0:T(8,128)(2,1)S(1)} %copy-done.1, bf16[2,1280,128]{2,1,0:T(8,128)(2,1)S(1)} %copy-done.4, ...), custom_call_target="tpu_custom_call" | custom-call | tf_op jit(solution)/shard_map/fetch/pallas_call | solution.py:534
  29.6 0.0 copy-start.3
  29.6 1.5 %copy-done.3 = bf16[32,160,256]{2,1,0:T(8,128)(2,1)} copy-done((bf16[32,160,256]{2,1,0:T(8,128)(2,1)}, bf16[32,160,256]{2,1,0:T(8,128)(2,1)S(1)}, u32[]{:S(2)}) %copy-start.3) | copy-done | bytes 2621464
  31.1 0.0 copy-start.5
  31.1 0.7 copy-done.5
  31.9 0.0 copy-start.8
  31.9 0.6 copy-done.8
  32.5 9.3 %attend.1 = (bf16[160,1024]{1,0:T(8,128)(2,1)}, bf16[160,1024]{1,0:T(8,128)(2,1)}, bf16[2,16,160,256]{3,2,1,0:T(8,128)(2,1)}, f32[160,256]{1,0:T(8,128)}, f32[8,256]{1,0:T(8,128)}) custom-call(s32[32]{0:T(128)} %counts.1, bf16[32,160,256]{2,1,0:T(8,128)(2,1)} %copy-done.3, bf16[1280,128]{1,0:T(8,128)(2,1)} %bitcast.2, bf16[160,1024]{1,0:T(8,128)(2,1)} %g.1, ...), custom_call_target="tpu_custom_call" | custom-call | tf_op jit(solution)/shard_map/attend/pallas_call | solution.py:553
  41.8 0.0 copy-start.2
  41.8 1.7 %copy-done.2 = bf16[2,16,160,256]{3,2,1,0:T(8,128)(2,1)S(1)} copy-done((bf16[2,16,160,256]{3,2,1,0:T(8,128)(2,1)S(1)}, bf16[2,16,160,256]{3,2,1,0:T(8,128)(2,1)}, u32[]{:S(2)}) %copy-start.2) | copy-done | bytes 2621464
  43.5 0.9 copy-done.6
  44.4 0.7 copy-done.7
  45.1 51.4 %settle.1 = (bf16[2,160,128]{2,1,0:T(8,128)(2,1)S(1)}, f32[8,128]{1,0:T(8,128)S(1)}) custom-call(bf16[2,16,160,256]{3,2,1,0:T(8,128)(2,1)S(1)} %copy-done.2, f32[160,256]{1,0:T(8,128)S(1)} %copy-done.6, f32[8,256]{1,0:T(8,128)S(1)} %copy-done.7, bf16[160,1024]{1,0:T(8,128)(2,1)S(1)} %get-tuple-element.23.x), custom_call_target="tpu_custom_call" | custom-call | tf_op jit(solution)/shard_map/settle/pallas_call | solution.py:569
  96.5 0.6 copy.13
  97.1 0.6 copy.14
  (2 shorter events, 0.0 us)
Async XLA Ops:
  1.3 1.7 %copy-start = (bf16[1280,1024]{1,0:T(8,128)(2,1)S(1)}, bf16[1280,1024]{1,0:T(8,128)(2,1)}, u32[]{:S(2)}) copy-start(bf16[1280,1024]{1,0:T(8,128)(2,1)} %hid.1) | copy-start | bytes 7864324
  3.1 1.7 %copy-start.1 = (bf16[1280,1024]{1,0:T(8,128)(2,1)S(1)}, bf16[1280,1024]{1,0:T(8,128)(2,1)}, u32[]{:S(2)}) copy-start(bf16[1280,1024]{1,0:T(8,128)(2,1)} %qry.1) | copy-start | bytes 7864324
  4.8 1.1 %copy-start.4 = (bf16[2,1280,128]{2,1,0:T(8,128)(2,1)S(1)}, bf16[2,1280,128]{2,1,0:T(8,128)(2,1)}, u32[]{:S(2)}) copy-start(bf16[2,1280,128]{2,1,0:T(8,128)(2,1)} %kv.1) | copy-start | bytes 1966084
  5.9 0.7 copy-start.9
  29.6 1.5 %copy-start.3 = (bf16[32,160,256]{2,1,0:T(8,128)(2,1)}, bf16[32,160,256]{2,1,0:T(8,128)(2,1)S(1)}, u32[]{:S(2)}) copy-start(bf16[32,160,256]{2,1,0:T(8,128)(2,1)S(1)} %get-tuple-element.15.kvall) | copy-start | bytes 7864324
  31.1 0.7 copy-start.5
  31.9 0.6 copy-start.8
  41.8 1.7 %copy-start.2 = (bf16[2,16,160,256]{3,2,1,0:T(8,128)(2,1)S(1)}, bf16[2,16,160,256]{3,2,1,0:T(8,128)(2,1)}, u32[]{:S(2)}) copy-start(bf16[2,16,160,256]{3,2,1,0:T(8,128)(2,1)} %get-tuple-element.20.contrib) | copy-start | bytes 7864324
  43.5 0.9 copy-start.6
  44.4 0.7 copy-start.7

commit v2 on v1

--- a/solution.py
+++ b/solution.py
@@ -11,6 +11,7 @@
 HEAD_WIDTH = 128
 MESH = pl.DeviceIdType.MESH
 NEG = -1e30
+VMEM_LIMIT = 62 * 2 ** 20
 CHUNK = 256
 LIVE_SHARE = (5, 8)
 F32 = jnp.float32
@@ -34,7 +35,7 @@
 
 
 def fetch_kernel(nseq, ntp, hid, qry, kv, w, routed, x_out, q_out, kvall, logit_out,
-                 hid_v, qry_v, kv_v, part, lsem, ssem, rsem, fsem, gsem, tssem, trsem):
+                 hid_v, qry_v, kv_v, held, part, lsem, ssem, rsem, fsem, gsem, tssem, trsem):
     me, mt = lax.axis_index("seq"), lax.axis_index("tp")
     nchip = nseq // 2
     chip, core = me // 2, me % 2
@@ -73,14 +74,16 @@
         [jnp.where(col == lane + 128.0 * j, 1.0, 0.0).astype(BF16) for j in range(tok // 128)], axis=1
     )
     load_kv.wait()
-    kvall[me, :, 0:128] = dot_nn(onehot, kv_v[0]).astype(BF16)
-    kvall[me, :, 128:256] = dot_nn(onehot, kv_v[1]).astype(BF16)
+    held[:, 0:128] = dot_nn(onehot, kv_v[0]).astype(BF16)
+    held[:, 128:256] = dot_nn(onehot, kv_v[1]).astype(BF16)
+    keep = pltpu.make_async_copy(held, kvall.at[me], lsem.at[3])
+    keep.start()
 
     pl.semaphore_wait(barrier, nchip - 1 - chip + 1 + ntp - 1)
 
     def to_chip(c):
         return pltpu.make_async_remote_copy(
-            src_ref=kvall.at[me], dst_ref=kvall.at[me], send_sem=ssem.at[c], recv_sem=rsem.at[chip],
+            src_ref=held, dst_ref=kvall.at[me], send_sem=ssem.at[c], recv_sem=rsem.at[chip],
             device_id={"seq": 2 * c + core}, device_id_type=MESH)
 
     def send_chip(i, _):
@@ -93,7 +96,7 @@
 
     def own_to_sib():
         return pltpu.make_async_remote_copy(
-            src_ref=kvall.at[me], dst_ref=kvall.at[me], send_sem=fsem.at[chip], recv_sem=gsem.at[chip],
+            src_ref=held, dst_ref=kvall.at[me], send_sem=fsem.at[chip], recv_sem=gsem.at[chip],
             device_id={"seq": sib}, device_id_type=MESH)
 
     lax.fori_loop(0, nchip, send_chip, 0)
@@ -184,6 +187,7 @@
         return 0
 
     lax.fori_loop(0, nchip, finish, 0)
+    keep.wait()
 
     @pl.when(core == 0)
     def _():
@@ -202,24 +206,42 @@
     lax.fori_loop(0, ntp, finish_tp, 0)
 
 
-def attend_kernel(scale, counts, kvall, q, g, logit, branch, dq, contrib, own, gterm,
-                  kx, vx, qtx, dotx, dob, s_scr, e_scr, ot, wide, dkv):
+def attend_kernel(scale, counts, kv_hbm, q_hbm, g_hbm, logit, branch, dq, contrib_hbm, own, gterm,
+                  kvall, q, g, contrib, lsem, csem, kx, vx, qtx, dotx, dob, s_scr, e_scr, ot, wide, dkv):
     me = lax.axis_index("seq")
     cap, width = g.shape
     nq = q.shape[0]
     heads = width // 128
     to_exp2 = scale * math.log2(math.e)
     live_here = counts[me]
+    loads = [
+        pltpu.make_async_copy(kv_hbm.at[me], kvall.at[me], lsem.at[0]),
+        pltpu.make_async_copy(q_hbm, q, lsem.at[1]),
+        pltpu.make_async_copy(g_hbm, g, lsem.at[2]),
+    ]
+    for load in loads:
+        load.start()
+
+    def block_load(s):
+        return pltpu.make_async_copy(kv_hbm.at[s], kvall.at[s], csem.at[s])
+
+    def start_load(s, _):
+        block_load(s).start()
+        return 0
+
+    lax.fori_loop(0, me, start_load, 0)
 
     row = lax.broadcasted_iota(jnp.int32, (cap, 128), 0)
     lane = lax.broadcasted_iota(jnp.int32, (cap, 128), 1)
     ones3 = jnp.where(lane < 3, 1.0, 0.0).astype(BF16)
+    loads[0].wait()
     kx[0:cap, 0:128] = kvall[me, :, 0:128]
     kx[0:cap, 128:256] = jnp.zeros((cap, 128), BF16)
     vx[0:cap, 0:128] = kvall[me, :, 128:256]
     vx[0:cap, 128:256] = ones3
 
     def place(s, off):
+        block_load(s).wait()
         off = pl.multiple_of(off, 16)
         n = counts[s]
         kx[pl.ds(off, cap), 0:128] = kvall[s, :, 0:128]
@@ -234,9 +256,16 @@
         lax.broadcasted_iota(jnp.int32, (CHUNK, 128), 1) == 0, NEG, 0.0).astype(BF16)
     vx[pl.ds(end, CHUNK), :] = jnp.zeros((CHUNK, 256), BF16)
     chunks = (end - cap + CHUNK - 1) // CHUNK
-
-    def at(c):
-        return pl.ds(pl.multiple_of(cap + c * CHUNK, 32), CHUNK)
+    doubles = chunks // 2
+
+    def at(c, size):
+        return pl.ds(pl.multiple_of(cap + c * CHUNK, 32), size * CHUNK)
+
+    def sweep(step, carry):
+        carry = lax.fori_loop(0, doubles, lambda c, held: step(at(2 * c, 2), 2 * CHUNK, held), carry)
+        return lax.fori_loop(2 * doubles, chunks, lambda c, held: step(at(c, 1), CHUNK, held), carry)
+
+    loads[1].wait()
 
     qtx[0:128, :] = q[...].T
     first = lax.broadcasted_iota(jnp.int32, (128, nq), 0)
@@ -251,12 +280,12 @@
     s_scr[0:cap, :] = s
     top = jnp.max(s.reshape(cap // 8, 8, nq), axis=0)
 
-    def score(c, top):
-        s = dot_nn(kx[at(c), :], qtx[...])
-        s_scr[at(c), :] = s
-        return jnp.maximum(top, jnp.max(s.reshape(CHUNK // 8, 8, nq), axis=0))
-
-    top = lax.fori_loop(0, chunks, score, top)
+    def score(sl, rows, top):
+        s = dot_nn(kx[sl, :], qtx[...])
+        s_scr[sl, :] = s
+        return jnp.maximum(top, jnp.max(s.reshape(rows // 8, 8, nq), axis=0))
+
+    top = sweep(score, top)
     top = jnp.max(top, axis=0, keepdims=True) * to_exp2
 
     def soften(sl, rows, total, start):
@@ -268,7 +297,7 @@
         return total + jnp.sum(e.reshape(rows // 8, 8, nq), axis=0)
 
     total = soften(pl.ds(0, cap), cap, jnp.zeros((8, nq), F32), True)
-    total = lax.fori_loop(0, chunks, lambda c, t: soften(at(c), CHUNK, t, False), total)
+    total = sweep(lambda sl, rows, t: soften(sl, rows, t, False), total)
     inverse = 1.0 / jnp.sum(total, axis=0, keepdims=True)
 
     z = logit[0:1, 0:cap]
@@ -278,6 +307,7 @@
     factor = jnp.where(live, gate * (1.0 - gate), 0.0)
     ot[...] = ot[...] * inverse
     wide[...] = ot[...].T
+    loads[2].wait()
     acc = jnp.zeros((cap, 128), F32)
     for h in range(heads):
         rows, lanes = slice(h * cap, (h + 1) * cap), slice(h * 128, (h + 1) * 128)
@@ -302,7 +332,7 @@
 
     def back(sl, start):
         e = e_scr[sl, :]
-        ds = (e.astype(F32) * dot_nn(vx[sl, :], dotx[...])).astype(BF16)
+        ds = e * dot_nn(vx[sl, :], dotx[...]).astype(BF16)
         add = dot_tn(kx[sl, 0:128], ds)
         wide_t = ot
         wide_t[...] = add if start else wide_t[...] + add
@@ -312,38 +342,54 @@
     own[:, 0:128] = dk
     own[:, 128:256] = dv
 
-    def back_chunk(c, _):
-        dk, dv = back(at(c), False)
-        dkv[at(c), 0:128] = dk.astype(BF16)
-        dkv[at(c), 128:256] = dv.astype(BF16)
-        return 0
-
-    lax.fori_loop(0, chunks, back_chunk, 0)
-
-    wide[...] = (ot[...] * scale).T
-    for h in range(heads):
-        dq[:, h * 128:(h + 1) * 128] = wide[h * cap:(h + 1) * cap, :].astype(BF16)
-
+    def back_chunk(sl, rows, _):
+        dk, dv = back(sl, False)
+        dkv[sl, 0:128] = dk.astype(BF16)
+        dkv[sl, 128:256] = dv.astype(BF16)
+        return 0
+
+    sweep(back_chunk, 0)
     row2 = lax.broadcasted_iota(jnp.int32, (cap, 256), 0)
+
+    def block_store(s):
+        return pltpu.make_async_copy(contrib.at[s % 2, s // 2], contrib_hbm.at[s % 2, s // 2], csem.at[s])
 
     def unplace(s, off):
         off = pl.multiple_of(off, 16)
         n = counts[s]
         block = dkv[pl.ds(off, cap), :].astype(F32)
         contrib[s % 2, s // 2] = jnp.where(row2 < n, block, 0.0).astype(BF16)
+        block_store(s).start()
         return off + ((n + 15) // 16) * 16
 
     lax.fori_loop(0, me, unplace, cap)
 
-
-def return_kernel(nseq, ntp, contrib, own, gterm, x, dkv_out, router_out,
-                  pair, mine, inbox, part, gpair, gchip, sums, psem, prsem, ssem, rsem, tssem, trsem,
+    wide[...] = (ot[...] * scale).T
+    for h in range(heads):
+        dq[:, h * 128:(h + 1) * 128] = wide[h * cap:(h + 1) * cap, :].astype(BF16)
+
+    def finish_store(s, _):
+        block_store(s).wait()
+        return 0
+
+    lax.fori_loop(0, me, finish_store, 0)
+
+
+def return_kernel(nseq, ntp, contrib, own_hbm, gterm, x_hbm, dkv_out, router_out,
+                  half, own, x, lsem, pair, mine, inbox, part, gpair, gchip, sums, psem, prsem, ssem, rsem, tssem, trsem,
                   qsem, qrsem, gssem, grsem):
     me, mt = lax.axis_index("seq"), lax.axis_index("tp")
     nchip = nseq // 2
     chip, core = me // 2, me % 2
     sib = me + 1 - 2 * core
     cap = x.shape[0]
+    loads = [
+        pltpu.make_async_copy(contrib.at[core], half, lsem.at[0]),
+        pltpu.make_async_copy(own_hbm, own, lsem.at[1]),
+        pltpu.make_async_copy(x_hbm, x, lsem.at[2]),
+    ]
+    for load in loads:
+        load.start()
 
     barrier = pltpu.get_barrier_semaphore()
 
@@ -396,11 +442,13 @@
             src_ref=mine.at[c], dst_ref=inbox.at[chip], send_sem=ssem.at[c], recv_sem=rsem.at[chip],
             device_id={"seq": 2 * c + core}, device_id_type=MESH)
 
+    loads[0].wait()
+
     def join(c, _):
         @pl.when(c < chip)
         def _():
             pair_copy(c).wait_recv()
-            mine[c] = (contrib[core, c].astype(F32) + pair[c].astype(F32)).astype(BF16)
+            mine[c] = (half[c].astype(F32) + pair[c].astype(F32)).astype(BF16)
             chip_copy(c).start()
         return 0
 
@@ -421,6 +469,7 @@
     r1 = dlogit - p1.astype(F32)
     p2 = r1.astype(BF16)
     p3 = (r1 - p2.astype(F32)).astype(BF16)
+    loads[2].wait()
     xs = x[...]
     share = (dot_nn(jnp.broadcast_to(p1, (16, cap)), xs) + dot_nn(jnp.broadcast_to(p2, (16, cap)), xs)
              + dot_nn(jnp.broadcast_to(p3, (16, cap)), xs))
@@ -463,6 +512,7 @@
             src_ref=inbox.at[c], dst_ref=inbox.at[c], send_sem=ssem.at[c], recv_sem=rsem.at[c],
             device_id={"seq": 2 * c + core}, device_id_type=MESH)
 
+    loads[1].wait()
     sums[...] = own[...] + pair[nchip].astype(F32)
 
     def add(c, _):
@@ -536,14 +586,14 @@
         out_shape=(shape((cap, width), BF16), shape((heads, cap, 128), BF16),
                    shape((nseq, cap, 256), BF16), shape((8, 256), F32)),
         in_specs=[anywhere] * 3 + vmem(2),
-        out_specs=tuple(vmem(4)),
+        out_specs=tuple(vmem(2)) + (anywhere, vmem()),
         scratch_shapes=[
             pltpu.VMEM((tok, width), BF16), pltpu.VMEM((tok, width), BF16), pltpu.VMEM((2, tok, 128), BF16),
-            pltpu.VMEM((ntp, 8, 256), F32), dma((3,)), dma((nchip,)), dma((nchip,)), dma((nchip,)),
+            pltpu.VMEM((cap, 256), BF16), pltpu.VMEM((ntp, 8, 256), F32), dma((4,)), dma((nchip,)), dma((nchip,)), dma((nchip,)),
             dma((nchip,)), dma((ntp,)), dma((ntp,)),
         ],
         compiler_params=pltpu.CompilerParams(
-            collective_id=0, has_side_effects=True, vmem_limit_bytes=40 * 2 ** 20),
+            collective_id=0, has_side_effects=True, vmem_limit_bytes=VMEM_LIMIT),
         name="fetch",
     )(hidden, queries, keys_values, w_router.reshape(1, width), routed)
 
@@ -554,24 +604,27 @@
         functools.partial(attend_kernel, scale),
         out_shape=(shape((cap, width), BF16), shape((cap, width), BF16),
                    shape((2, nchip, cap, 256), BF16), shape((cap, 256), F32), shape((8, 256), F32)),
-        in_specs=[pl.BlockSpec(memory_space=pltpu.SMEM)] + vmem(4),
-        out_specs=tuple(vmem(5)),
+        in_specs=[pl.BlockSpec(memory_space=pltpu.SMEM)] + [anywhere] * 3 + [vmem()],
+        out_specs=tuple(vmem(2)) + (anywhere,) + tuple(vmem(2)),
         scratch_shapes=[
+            pltpu.VMEM((nseq, cap, 256), BF16), pltpu.VMEM((nq, 128), BF16), pltpu.VMEM((cap, width), BF16),
+            pltpu.VMEM((2, nchip, cap, 256), BF16), dma((3,)), dma((nseq,)),
             pltpu.VMEM((rows, 256), BF16), pltpu.VMEM((rows, 256), BF16),
             pltpu.VMEM((256, nq), BF16), pltpu.VMEM((256, nq), BF16), pltpu.VMEM((nq, 128), BF16),
             pltpu.VMEM((cap + span, nq), F32), pltpu.VMEM((cap + span, nq), BF16),
             pltpu.VMEM((128, nq), F32), pltpu.VMEM((nq, 128), F32), pltpu.VMEM((rows, 256), BF16),
         ],
-        compiler_params=pltpu.CompilerParams(vmem_limit_bytes=60 * 2 ** 20),
+        compiler_params=pltpu.CompilerParams(vmem_limit_bytes=VMEM_LIMIT),
         name="attend",
     )(counts, kvall, q.reshape(nq, 128), grad_out, logit)
 
     dkv, router = pl.pallas_call(
         functools.partial(return_kernel, nseq, ntp),
         out_shape=(shape((2, cap, 128), BF16), shape((8, 128), F32)),
-        in_specs=vmem(4),
+        in_specs=[anywhere, anywhere, vmem(), anywhere],
         out_specs=tuple(vmem(2)),
         scratch_shapes=[
+            pltpu.VMEM((nchip, cap, 256), BF16), pltpu.VMEM((cap, 256), F32), pltpu.VMEM((cap, width), BF16), dma((3,)),
             pltpu.VMEM((nchip + 1, cap, 256), BF16), pltpu.VMEM((nchip, cap, 256), BF16),
             pltpu.VMEM((nchip, cap, 256), BF16), pltpu.VMEM((ntp, 8, 256), F32),
             pltpu.VMEM((2, 8, 128), F32), pltpu.VMEM((nchip, 8, 128), F32), pltpu.VMEM((cap, 256), F32),
@@ -579,7 +632,7 @@
             dma, dma, dma((nchip,)), dma((nchip,)),
         ],
         compiler_params=pltpu.CompilerParams(
-            collective_id=1, has_side_effects=True, vmem_limit_bytes=40 * 2 ** 20),
+            collective_id=1, has_side_effects=True, vmem_limit_bytes=VMEM_LIMIT),
         name="settle",
     )(contrib, own, gterm, x)
     return branch, dq, dkv, router.reshape(8 * 128)

time: 98.1 us -> 88.3 us (0.900)
  local copies, waits for them, and re-layouts: 13.4 us -> 4.08 us
    unnamed x22 -> x2, local copies, waits for them, and re-layouts: 12.7 us -> 2.8 us
    pallas_call x1, Pallas kernels: 51.4 us -> 49 us  [shards(): pl.pallas_call(functools.partial(return_kernel, nseq, ntp), out_shape=(sh...]
where the time goes in v2:
time: 88.3 us; the launch traced here: 87.9 us
  Pallas kernels  83.2 us (94%)
  local copies, waits for them, and re-layouts  4.08 us (5%)
    pallas_call x1, Pallas kernels, shards(): pl.pallas_call(functools.partial(return_kernel, nseq, ntp), out_shape=(sh...  49 us
    pallas_call x1, Pallas kernels, shards(): pl.pallas_call(functools.partial(fetch_kernel, nseq, ntp), out_shape=(sha...  23.8 us
    pallas_call x1, Pallas kernels, shards(): pl.pallas_call(functools.partial(attend_kernel, scale), out_shape=(shape(...  10.3 us
    unnamed x2, local copies, waits for them, and re-layouts  2.8 us

profile of v2, /device:TPU:24, one launch (start us, length us, event | category | flops | bytes accessed | tf_op | source)
XLA Modules:
  0.0 87.9 jit_solution(5311264702869173997)
XLA Ops:
  0.6 1.3 %reshape.17.w = bf16[1,1024]{1,0:T(2,128)(2,1)} reshape(bf16[1024]{0:T(1024)(128)(2,1)} %param.10) | data formatting | bytes 4096 | tf_op jit(solution)/shard_map/reshape | solution.py:598
  1.9 23.8 %fetch.1 = (bf16[160,1024]{1,0:T(8,128)(2,1)}, bf16[8,160,128]{2,1,0:T(8,128)(2,1)}, bf16[32,160,256]{2,1,0:T(8,128)(2,1)}, f32[8,256]{1,0:T(8,128)}) custom-call(bf16[1280,1024]{1,0:T(8,128)(2,1)} %hid.1, bf16[1280,1024]{1,0:T(8,128)(2,1)} %qry.1, bf16[2,1280,128]{2,1,0:T(8,128)(2,1)} %kv.1, bf16[1,1024]{1,0:T(2,128)(2,1)} %reshape.17.w, s32[1,160]{1,0:T(1,128)} %routed.1), custom_call_target="tpu_custom_call" | custom-call | tf_op jit(solution)/shard_map/fetch/pallas_call | solution.py:584
  25.8 10.3 %attend.1 = (bf16[160,1024]{1,0:T(8,128)(2,1)}, bf16[160,1024]{1,0:T(8,128)(2,1)}, bf16[2,16,160,256]{3,2,1,0:T(8,128)(2,1)}, f32[160,256]{1,0:T(8,128)}, f32[8,256]{1,0:T(8,128)}) custom-call(s32[32]{0:T(128)} %counts.1, bf16[32,160,256]{2,1,0:T(8,128)(2,1)} %get-tuple-element.15.kv_hbm, bf16[1280,128]{1,0:T(8,128)(2,1)} %bitcast.2, ...), custom_call_target="tpu_custom_call" | custom-call | tf_op jit(solution)/shard_map/attend/pallas_call | solution.py:603
  36.1 49.0 %settle.1 = (bf16[2,160,128]{2,1,0:T(8,128)(2,1)}, f32[8,128]{1,0:T(8,128)}) custom-call(bf16[2,16,160,256]{3,2,1,0:T(8,128)(2,1)} %get-tuple-element.20.contrib, f32[160,256]{1,0:T(8,128)} %get-tuple-element.21.own_hbm, f32[8,256]{1,0:T(8,128)} %get-tuple-element.22.gterm, bf16[160,1024]{1,0:T(8,128)(2,1)} %get-tuple-element.23.x_hbm), custom_call_target="tpu_custom_call" | custom-call | tf_op jit(solution)/shard_map/settle/pallas_call | solution.py:621
  85.1 1.5 %copy.13 = bf16[2,160,128]{2,1,0:T(8,128)(2,1)} copy(bf16[2,160,128]{2,1,0:T(8,128)(2,1)} %get-tuple-element.32) | data formatting | bytes 163840
  86.6 1.3 %copy.14 = f32[1024]{0:T(1024)} copy(f32[1024]{0:T(1024)} %bitcast.3) | data formatting | bytes 8192

commit v3 on v2

--- a/solution.py
+++ b/solution.py
@@ -34,8 +34,24 @@
     return jnp.broadcast_to(row, (128, cap)).T
 
 
+class Grid:
+    def __init__(self, me, nchip):
+        self.side = math.isqrt(nchip)
+        self.chip, self.core = me // 2, me % 2
+        self.sib = me + 1 - 2 * self.core
+        high, low = self.chip // self.side, self.chip % self.side
+        self.a = jnp.where(self.core == 0, high, low)
+        self.b = jnp.where(self.core == 0, low, high)
+
+    def at(self, a, b):
+        return jnp.where(self.core == 0, self.side * a + b, self.side * b + a)
+
+    def device(self, chip):
+        return {"seq": 2 * chip + self.core}
+
+
 def fetch_kernel(nseq, ntp, hid, qry, kv, w, routed, x_out, q_out, kvall, logit_out,
-                 hid_v, qry_v, kv_v, held, part, lsem, ssem, rsem, fsem, gsem, tssem, trsem):
+                 hid_v, qry_v, kv_v, held, part, lsem, ssem, ssem2, rsem, fsem, gsem, tssem, trsem):
     me, mt = lax.axis_index("seq"), lax.axis_index("tp")
     nchip = nseq // 2
     chip, core = me // 2, me % 2
@@ -52,11 +68,16 @@
 
     barrier = pltpu.get_barrier_semaphore()
 
-    def greet_chip(c, _):
-        @pl.when(c < chip)
-        def _():
-            pl.semaphore_signal(barrier, inc=1, device_id={"seq": 2 * c + core}, device_id_type=MESH)
-        return 0
+    grid = Grid(me, nchip)
+    side, last = grid.side, grid.side - 1
+    for q in range(side):
+        @pl.when(q != grid.b)
+        def _():
+            pl.semaphore_signal(barrier, inc=1, device_id=grid.device(grid.at(grid.a, q)), device_id_type=MESH)
+
+        @pl.when(q != grid.a)
+        def _():
+            pl.semaphore_signal(barrier, inc=1, device_id=grid.device(grid.at(q, grid.b)), device_id_type=MESH)
 
     def greet_tp(t, _):
         @pl.when(t != mt)
@@ -64,7 +85,6 @@
             pl.semaphore_signal(barrier, inc=1, device_id={"tp": t}, device_id_type=MESH)
         return 0
 
-    lax.fori_loop(0, nchip, greet_chip, 0)
     pl.semaphore_signal(barrier, inc=1, device_id={"seq": sib}, device_id_type=MESH)
     lax.fori_loop(0, ntp, greet_tp, 0)
 
@@ -79,31 +99,67 @@
     keep = pltpu.make_async_copy(held, kvall.at[me], lsem.at[3])
     keep.start()
 
-    pl.semaphore_wait(barrier, nchip - 1 - chip + 1 + ntp - 1)
-
-    def to_chip(c):
-        return pltpu.make_async_remote_copy(
-            src_ref=held, dst_ref=kvall.at[me], send_sem=ssem.at[c], recv_sem=rsem.at[chip],
-            device_id={"seq": 2 * c + core}, device_id_type=MESH)
-
-    def send_chip(i, _):
-        c = nchip - 1 - i
-
-        @pl.when(c > chip)
-        def _():
-            to_chip(c).start()
-        return 0
+    pl.semaphore_wait(barrier, 2 * last + 1 + ntp - 1)
+
+    def to_line(q):
+        return pltpu.make_async_remote_copy(
+            src_ref=held, dst_ref=kvall.at[me], send_sem=ssem.at[q], recv_sem=rsem.at[chip],
+            device_id=grid.device(grid.at(grid.a, q)), device_id_type=MESH)
+
+    def line_used(q):
+        return (q != grid.b) & (chip < grid.at(last, q))
 
     def own_to_sib():
         return pltpu.make_async_remote_copy(
             src_ref=held, dst_ref=kvall.at[me], send_sem=fsem.at[chip], recv_sem=gsem.at[chip],
             device_id={"seq": sib}, device_id_type=MESH)
 
-    lax.fori_loop(0, nchip, send_chip, 0)
+    def across(p, q):
+        c = grid.at(grid.a, q)
+        block = kvall.at[2 * c + core]
+        return pltpu.make_async_remote_copy(
+            src_ref=block, dst_ref=block, send_sem=ssem2.at[p * side + q], recv_sem=rsem.at[c],
+            device_id=grid.device(grid.at(p, grid.b)), device_id_type=MESH)
+
+    def own_across(p):
+        return pltpu.make_async_remote_copy(
+            src_ref=held, dst_ref=kvall.at[me], send_sem=ssem2.at[p * side + grid.b], recv_sem=rsem.at[chip],
+            device_id=grid.device(grid.at(p, grid.b)), device_id_type=MESH)
+
+    def across_used(p, q):
+        return (p != grid.a) & (grid.at(grid.a, q) < grid.at(p, grid.b))
+
+    for q in range(side):
+        @pl.when(line_used(q))
+        def _():
+            to_line(q).start()
+
+    for p in range(side):
+        @pl.when(across_used(p, grid.b))
+        def _():
+            own_across(p).start()
 
     @pl.when(core == 0)
     def _():
         own_to_sib().start()
+
+    def landed(c):
+        block = kvall.at[2 * c + core]
+        return pltpu.make_async_remote_copy(
+            src_ref=block, dst_ref=block, send_sem=fsem.at[c], recv_sem=rsem.at[c],
+            device_id={"seq": sib}, device_id_type=MESH)
+
+    def forward(c):
+        block = kvall.at[2 * c + core]
+        return pltpu.make_async_remote_copy(
+            src_ref=block, dst_ref=block, send_sem=fsem.at[c], recv_sem=gsem.at[c],
+            device_id={"seq": sib}, device_id_type=MESH)
+
+    def forwarded(c):
+        block = kvall.at[2 * c + 1 - core]
+        return pltpu.make_async_remote_copy(
+            src_ref=block, dst_ref=block, send_sem=fsem.at[c], recv_sem=gsem.at[c],
+            device_id={"seq": sib}, device_id_type=MESH)
 
     load_hid.wait()
     x = dot_nn(onehot, hid_v[...]).astype(BF16)
@@ -130,6 +186,22 @@
 
     lax.fori_loop(0, ntp, send_tp, 0)
 
+    for q in range(side):
+        c = grid.at(grid.a, q)
+
+        @pl.when((q != grid.b) & (c < grid.at(last, grid.b)))
+        def _():
+            landed(c).wait_recv()
+
+            for p in range(side):
+                @pl.when(across_used(p, q))
+                def _():
+                    across(p, q).start()
+
+            @pl.when(c < chip)
+            def _():
+                forward(c).start()
+
     load_qry.wait()
     for h in range(heads):
         q_out[h] = dot_nn(onehot, qry_v[:, h * 128:(h + 1) * 128]).astype(BF16)
@@ -146,47 +218,32 @@
         total = total + part[t]
     logit_out[...] = total
 
-    def landed(c):
-        block = kvall.at[2 * c + core]
-        return pltpu.make_async_remote_copy(
-            src_ref=block, dst_ref=block, send_sem=fsem.at[c], recv_sem=rsem.at[c],
-            device_id={"seq": sib}, device_id_type=MESH)
-
-    def forward(c):
-        block = kvall.at[2 * c + core]
-        return pltpu.make_async_remote_copy(
-            src_ref=block, dst_ref=block, send_sem=fsem.at[c], recv_sem=gsem.at[c],
-            device_id={"seq": sib}, device_id_type=MESH)
-
-    def forwarded(c):
-        block = kvall.at[2 * c + 1 - core]
-        return pltpu.make_async_remote_copy(
-            src_ref=block, dst_ref=block, send_sem=fsem.at[c], recv_sem=gsem.at[c],
-            device_id={"seq": sib}, device_id_type=MESH)
-
-    def pass_on(i, _):
-        c = chip - 1 - i
-
-        @pl.when(c >= 0)
-        def _():
-            landed(c).wait_recv()
-            forward(c).start()
-        return 0
-
-    lax.fori_loop(0, nchip, pass_on, 0)
+    for step in range(1, side):
+        for q in range(side):
+            c = grid.at(lax.rem(grid.a - step + side, side), q)
+
+            @pl.when(c < chip)
+            def _():
+                landed(c).wait_recv()
+                forward(c).start()
 
     def finish(c, _):
         @pl.when(c < chip)
         def _():
             forwarded(c).wait_recv()
             forward(c).wait_send()
-
-        @pl.when(c > chip)
-        def _():
-            to_chip(c).wait_send()
         return 0
 
     lax.fori_loop(0, nchip, finish, 0)
+    for q in range(side):
+        @pl.when(line_used(q))
+        def _():
+            to_line(q).wait_send()
+
+        for p in range(side):
+            @pl.when(across_used(p, q))
+            def _():
+                across(p, q).wait_send()
     keep.wait()
 
     @pl.when(core == 0)
@@ -376,7 +433,7 @@
 
 
 def return_kernel(nseq, ntp, contrib, own_hbm, gterm, x_hbm, dkv_out, router_out,
-                  half, own, x, lsem, pair, mine, inbox, part, gpair, gchip, sums, psem, prsem, ssem, rsem, tssem, trsem,
+                  half, own, x, lsem, pair, mine, inbox, inbox2, turn, part, gpair, gchip, sums, psem, prsem, ssem, rsem, s2sem, r2sem, tssem, trsem,
                   qsem, qrsem, gssem, grsem):
     me, mt = lax.axis_index("seq"), lax.axis_index("tp")
     nchip = nseq // 2
@@ -437,22 +494,46 @@
 
     lax.fori_loop(0, nchip, send_pair, 0)
 
-    def chip_copy(c):
-        return pltpu.make_async_remote_copy(
-            src_ref=mine.at[c], dst_ref=inbox.at[chip], send_sem=ssem.at[c], recv_sem=rsem.at[chip],
-            device_id={"seq": 2 * c + core}, device_id_type=MESH)
+    grid = Grid(me, nchip)
+    side, last = grid.side, grid.side - 1
+
+    def first_copy(p, q):
+        return pltpu.make_async_remote_copy(
+            src_ref=mine.at[grid.at(p, q)], dst_ref=inbox.at[grid.a, q], send_sem=ssem.at[p * side + q],
+            recv_sem=rsem.at[grid.a * side + q], device_id=grid.device(grid.at(p, grid.b)), device_id_type=MESH)
+
+    def first_landed(p, q):
+        return pltpu.make_async_remote_copy(
+            src_ref=inbox.at[p, q], dst_ref=inbox.at[p, q], send_sem=ssem.at[p * side + q],
+            recv_sem=rsem.at[p * side + q], device_id=grid.device(grid.at(p, grid.b)), device_id_type=MESH)
+
+    def second_copy(q):
+        return pltpu.make_async_remote_copy(
+            src_ref=turn.at[q], dst_ref=inbox2.at[grid.b], send_sem=s2sem.at[q], recv_sem=r2sem.at[grid.b],
+            device_id=grid.device(grid.at(grid.a, q)), device_id_type=MESH)
+
+    def second_landed(q):
+        return pltpu.make_async_remote_copy(
+            src_ref=inbox2.at[q], dst_ref=inbox2.at[q], send_sem=s2sem.at[q], recv_sem=r2sem.at[q],
+            device_id=grid.device(grid.at(grid.a, q)), device_id_type=MESH)
 
     loads[0].wait()
 
-    def join(c, _):
-        @pl.when(c < chip)
-        def _():
-            pair_copy(c).wait_recv()
-            mine[c] = (half[c].astype(F32) + pair[c].astype(F32)).astype(BF16)
-            chip_copy(c).start()
-        return 0
-
-    lax.fori_loop(0, nchip, join, 0)
+    def join(c):
+        pair_copy(c).wait_recv()
+        mine[c] = (half[c].astype(F32) + pair[c].astype(F32)).astype(BF16)
+
+    for p in range(side):
+        for q in range(side):
+            @pl.when((p != grid.a) & (grid.at(p, q) < chip))
+            def _():
+                join(grid.at(p, q))
+                first_copy(p, q).start()
+
+    for q in range(side):
+        @pl.when(grid.at(grid.a, q) < chip)
+        def _():
+            join(grid.at(grid.a, q))
 
     def wait_tp(t, _):
         @pl.when(t != mt)
@@ -473,7 +554,7 @@
     xs = x[...]
     share = (dot_nn(jnp.broadcast_to(p1, (16, cap)), xs) + dot_nn(jnp.broadcast_to(p2, (16, cap)), xs)
              + dot_nn(jnp.broadcast_to(p3, (16, cap)), xs))
-    for i in range(8):
+    for i in range(x.shape[1] // 128):
         gpair[core, i:i + 1, :] = share[0:1, i * 128:(i + 1) * 128]
 
     def gpair_copy(slot):
@@ -497,6 +578,27 @@
         return 0
 
     lax.fori_loop(0, nchip, send_gchip, 0)
+
+    for q in range(side):
+        target = grid.at(grid.a, q)
+
+        @pl.when((q != grid.b) & (target < grid.at(last, grid.b)))
+        def _():
+            @pl.when(target < chip)
+            def _():
+                sums[...] = mine[target].astype(F32)
+
+            @pl.when(target >= chip)
+            def _():
+                sums[...] = jnp.zeros((cap, 256), F32)
+
+            for p in range(side):
+                @pl.when((p != grid.a) & (target < grid.at(p, grid.b)))
+                def _():
+                    first_landed(p, q).wait_recv()
+                    sums[...] = sums[...] + inbox[p, q].astype(F32)
+            turn[q] = sums[...].astype(BF16)
+            second_copy(q).start()
 
     @pl.when(core == 0)
     def _():
@@ -507,22 +609,20 @@
     def _():
         pair[nchip] = jnp.zeros((cap, 256), BF16)
 
-    def inbox_copy(c):
-        return pltpu.make_async_remote_copy(
-            src_ref=inbox.at[c], dst_ref=inbox.at[c], send_sem=ssem.at[c], recv_sem=rsem.at[c],
-            device_id={"seq": 2 * c + core}, device_id_type=MESH)
-
     loads[1].wait()
     sums[...] = own[...] + pair[nchip].astype(F32)
 
-    def add(c, _):
-        @pl.when(c > chip)
-        def _():
-            inbox_copy(c).wait_recv()
-            sums[...] = sums[...] + inbox[c].astype(F32)
-        return 0
-
-    lax.fori_loop(0, nchip, add, 0)
+    for p in range(side):
+        @pl.when((p != grid.a) & (chip < grid.at(p, grid.b)))
+        def _():
+            first_landed(p, grid.b).wait_recv()
+            sums[...] = sums[...] + inbox[p, grid.b].astype(F32)
+
+    for q in range(side):
+        @pl.when((q != grid.b) & (chip < grid.at(last, q)))
+        def _():
+            second_landed(q).wait_recv()
+            sums[...] = sums[...] + inbox2[q].astype(F32)
     dkv_out[0] = sums[:, 0:128].astype(BF16)
     dkv_out[1] = sums[:, 128:256].astype(BF16)
 
@@ -545,16 +645,22 @@
         def _():
             pair_copy(c).wait_send()
 
-        @pl.when(c < chip)
-        def _():
-            chip_copy(c).wait_send()
-
         @pl.when(c != chip)
         def _():
             gchip_copy(chip, c).wait_send()
         return 0
 
     lax.fori_loop(0, nchip, finish, 0)
+
+    for q in range(side):
+        for p in range(side):
+            @pl.when((p != grid.a) & (grid.at(p, q) < chip))
+            def _():
+                first_copy(p, q).wait_send()
+
+        @pl.when((q != grid.b) & (grid.at(grid.a, q) < grid.at(last, grid.b)))
+        def _():
+            second_copy(q).wait_send()
 
     def finish_tp(t, _):
         @pl.when(t != mt)
@@ -573,6 +679,7 @@
 def shards(hidden, queries, keys_values, w_router, routed, counts, grad_out):
     nseq, ntp = lax.axis_size("seq"), lax.axis_size("tp")
     nchip = nseq // 2
+    side = math.isqrt(nchip)
     cap = routed.shape[1]
     tok, width = queries.shape
     heads = width // HEAD_WIDTH
@@ -589,7 +696,7 @@
         out_specs=tuple(vmem(2)) + (anywhere, vmem()),
         scratch_shapes=[
             pltpu.VMEM((tok, width), BF16), pltpu.VMEM((tok, width), BF16), pltpu.VMEM((2, tok, 128), BF16),
-            pltpu.VMEM((cap, 256), BF16), pltpu.VMEM((ntp, 8, 256), F32), dma((4,)), dma((nchip,)), dma((nchip,)), dma((nchip,)),
+            pltpu.VMEM((cap, 256), BF16), pltpu.VMEM((ntp, 8, 256), F32), dma((4,)), dma((nchip,)), dma((nchip,)), dma((nchip,)), dma((nchip,)),
             dma((nchip,)), dma((ntp,)), dma((ntp,)),
         ],
         compiler_params=pltpu.CompilerParams(
@@ -620,22 +727,23 @@
 
     dkv, router = pl.pallas_call(
         functools.partial(return_kernel, nseq, ntp),
-        out_shape=(shape((2, cap, 128), BF16), shape((8, 128), F32)),
+        out_shape=(shape((2, cap, 128), BF16), shape((width // 128, 128), F32)),
         in_specs=[anywhere, anywhere, vmem(), anywhere],
         out_specs=tuple(vmem(2)),
         scratch_shapes=[
             pltpu.VMEM((nchip, cap, 256), BF16), pltpu.VMEM((cap, 256), F32), pltpu.VMEM((cap, width), BF16), dma((3,)),
             pltpu.VMEM((nchip + 1, cap, 256), BF16), pltpu.VMEM((nchip, cap, 256), BF16),
-            pltpu.VMEM((nchip, cap, 256), BF16), pltpu.VMEM((ntp, 8, 256), F32),
-            pltpu.VMEM((2, 8, 128), F32), pltpu.VMEM((nchip, 8, 128), F32), pltpu.VMEM((cap, 256), F32),
-            dma((nchip,)), dma((nchip,)), dma((nchip,)), dma((nchip,)), dma((ntp,)), dma((ntp,)),
+            pltpu.VMEM((side, side, cap, 256), BF16), pltpu.VMEM((side, cap, 256), BF16),
+            pltpu.VMEM((side, cap, 256), BF16), pltpu.VMEM((ntp, 8, 256), F32),
+            pltpu.VMEM((2, width // 128, 128), F32), pltpu.VMEM((nchip, width // 128, 128), F32), pltpu.VMEM((cap, 256), F32),
+            dma((nchip,)), dma((nchip,)), dma((nchip,)), dma((nchip,)), dma((side,)), dma((side,)), dma((ntp,)), dma((ntp,)),
             dma, dma, dma((nchip,)), dma((nchip,)),
         ],
         compiler_params=pltpu.CompilerParams(
             collective_id=1, has_side_effects=True, vmem_limit_bytes=VMEM_LIMIT),
         name="settle",
     )(contrib, own, gterm, x)
-    return branch, dq, dkv, router.reshape(8 * 128)
+    return branch, dq, dkv, router.reshape(width)
 
 
 def solution(mesh):

time: 88.3 us -> 77 us (0.87)
  Pallas kernels: 83.2 us -> 72 us
    pallas_call x1, Pallas kernels: 49 us -> 41.5 us  [shards(): pl.pallas_call(functools.partial(return_kernel, nseq, ntp), out_shape=(sh...]
    pallas_call x1, Pallas kernels: 23.8 us -> 20.2 us  [shards(): pl.pallas_call(functools.partial(fetch_kernel, nseq, ntp), out_shape=(sha...]
where the time goes in v3:
time: 77 us; the launch traced here: 76.7 us
  Pallas kernels  72 us (94%)
  local copies, waits for them, and re-layouts  4.08 us (5%)
    pallas_call x1, Pallas kernels, shards(): pl.pallas_call(functools.partial(return_kernel, nseq, ntp), out_shape=(sh...  41.5 us
    pallas_call x1, Pallas kernels, shards(): pl.pallas_call(functools.partial(fetch_kernel, nseq, ntp), out_shape=(sha...  20.2 us
    pallas_call x1, Pallas kernels, shards(): pl.pallas_call(functools.partial(attend_kernel, scale), out_shape=(shape(...  10.3 us
    unnamed x2, local copies, waits for them, and re-layouts  2.8 us

profile of v3, /device:TPU:24, one launch (start us, length us, event | category | flops | bytes accessed | tf_op | source)
XLA Modules:
  0.0 76.7 jit_solution(8918656018560291011)
XLA Ops:
  0.6 1.3 %reshape.17.w = bf16[1,1024]{1,0:T(2,128)(2,1)} reshape(bf16[1024]{0:T(1024)(128)(2,1)} %param.10) | data formatting | bytes 4096 | tf_op jit(solution)/shard_map/reshape | solution.py:705
  1.9 20.2 %fetch.1 = (bf16[160,1024]{1,0:T(8,128)(2,1)}, bf16[8,160,128]{2,1,0:T(8,128)(2,1)}, bf16[32,160,256]{2,1,0:T(8,128)(2,1)}, f32[8,256]{1,0:T(8,128)}) custom-call(bf16[1280,1024]{1,0:T(8,128)(2,1)} %hid.1, bf16[1280,1024]{1,0:T(8,128)(2,1)} %qry.1, bf16[2,1280,128]{2,1,0:T(8,128)(2,1)} %kv.1, bf16[1,1024]{1,0:T(2,128)(2,1)} %reshape.17.w, s32[1,160]{1,0:T(1,128)} %routed.1), custom_call_target="tpu_custom_call" | custom-call | tf_op jit(solution)/shard_map/fetch/pallas_call | solution.py:691
  22.1 10.3 %attend.1 = (bf16[160,1024]{1,0:T(8,128)(2,1)}, bf16[160,1024]{1,0:T(8,128)(2,1)}, bf16[2,16,160,256]{3,2,1,0:T(8,128)(2,1)}, f32[160,256]{1,0:T(8,128)}, f32[8,256]{1,0:T(8,128)}) custom-call(s32[32]{0:T(128)} %counts.1, bf16[32,160,256]{2,1,0:T(8,128)(2,1)} %get-tuple-element.15.kv_hbm, bf16[1280,128]{1,0:T(8,128)(2,1)} %bitcast.2, ...), custom_call_target="tpu_custom_call" | custom-call | tf_op jit(solution)/shard_map/attend/pallas_call | solution.py:710
  32.4 41.5 %settle.1 = (bf16[2,160,128]{2,1,0:T(8,128)(2,1)}, f32[8,128]{1,0:T(8,128)}) custom-call(bf16[2,16,160,256]{3,2,1,0:T(8,128)(2,1)} %get-tuple-element.20.contrib, f32[160,256]{1,0:T(8,128)} %get-tuple-element.21.own_hbm, f32[8,256]{1,0:T(8,128)} %get-tuple-element.22.gterm, bf16[160,1024]{1,0:T(8,128)(2,1)} %get-tuple-element.23.x_hbm), custom_call_target="tpu_custom_call" | custom-call | tf_op jit(solution)/shard_map/settle/pallas_call | solution.py:728
  73.9 1.5 %copy.13 = bf16[2,160,128]{2,1,0:T(8,128)(2,1)} copy(bf16[2,160,128]{2,1,0:T(8,128)(2,1)} %get-tuple-element.32) | data formatting | bytes 163840
  75.4 1.3 %copy.14 = f32[1024]{0:T(1024)} copy(f32[1024]{0:T(1024)} %bitcast.3) | data formatting | bytes 8192

commit v4 on v3

--- a/solution.py
+++ b/solution.py
@@ -164,7 +164,7 @@
     load_hid.wait()
     x = dot_nn(onehot, hid_v[...]).astype(BF16)
     x_out[...] = x
-    logit = dot_nt(jnp.broadcast_to(w[...], (16, w.shape[1])), x)
+    logit = dot_nt(jnp.broadcast_to(w[...].reshape(1, w.shape[0]), (16, w.shape[0])), x)
     part[mt, :, :] = jnp.zeros((8, 256), F32)
     part[mt, :, 0:cap] = logit[0:8]
 
@@ -227,40 +227,49 @@
                 landed(c).wait_recv()
                 forward(c).start()
 
-    def finish(c, _):
-        @pl.when(c < chip)
-        def _():
-            forwarded(c).wait_recv()
-            forward(c).wait_send()
-        return 0
-
-    lax.fori_loop(0, nchip, finish, 0)
     for q in range(side):
         @pl.when(line_used(q))
         def _():
             to_line(q).wait_send()
 
+    keep.wait()
+
+    @pl.when(core == 0)
+    def _():
+        own_to_sib().wait_send()
+
+    def finish_tp(t, _):
+        @pl.when(t != mt)
+        def _():
+            to_tp(t).wait_send()
+        return 0
+
+    lax.fori_loop(0, ntp, finish_tp, 0)
+    for q in range(side):
         for p in range(side):
             @pl.when(across_used(p, q))
             def _():
                 across(p, q).wait_send()
-    keep.wait()
-
-    @pl.when(core == 0)
-    def _():
-        own_to_sib().wait_send()
+
+    def finish_send(c, _):
+        @pl.when(c < chip)
+        def _():
+            forward(c).wait_send()
+        return 0
+
+    def finish(c, _):
+        @pl.when(c < chip)
+        def _():
+            forwarded(c).wait_recv()
+        return 0
+
+    lax.fori_loop(0, nchip, finish_send, 0)
 
     @pl.when(core == 1)
     def _():
         forwarded(chip).wait_recv()
 
-    def finish_tp(t, _):
-        @pl.when(t != mt)
-        def _():
-            to_tp(t).wait_send()
-        return 0
-
-    lax.fori_loop(0, ntp, finish_tp, 0)
+    lax.fori_loop(0, nchip, finish, 0)
 
 
 def attend_kernel(scale, counts, kv_hbm, q_hbm, g_hbm, logit, branch, dq, contrib_hbm, own, gterm,
@@ -319,7 +328,10 @@
         return pl.ds(pl.multiple_of(cap + c * CHUNK, 32), size * CHUNK)
 
     def sweep(step, carry):
-        carry = lax.fori_loop(0, doubles, lambda c, held: step(at(2 * c, 2), 2 * CHUNK, held), carry)
+        quads = chunks // 4
+        carry = lax.fori_loop(0, quads, lambda c, held: step(at(4 * c, 4), 4 * CHUNK, held), carry)
+        carry = lax.fori_loop(
+            2 * quads, doubles, lambda c, held: step(at(2 * c, 2), 2 * CHUNK, held), carry)
         return lax.fori_loop(2 * doubles, chunks, lambda c, held: step(at(c, 1), CHUNK, held), carry)
 
     loads[1].wait()
@@ -563,6 +575,22 @@
             device_id={"seq": sib}, device_id_type=MESH)
 
     gpair_copy(core).start()
+
+    def finish_pair(c, _):
+        @pl.when((c < chip) | ((c == chip) & (core == 1)))
+        def _():
+            pair_copy(c).wait_send()
+        return 0
+
+    lax.fori_loop(0, nchip, finish_pair, 0)
+
+    def finish_tp(t, _):
+        @pl.when(t != mt)
+        def _():
+            tp_copy(mt, t).wait_send()
+        return 0
+
+    lax.fori_loop(0, ntp, finish_tp, 0)
     gpair_copy(1 - core).wait_recv()
     gchip[chip] = gpair[0] + gpair[1]
 
@@ -600,6 +628,20 @@
             turn[q] = sums[...].astype(BF16)
             second_copy(q).start()
 
+    for q in range(side):
+        for p in range(side):
+            @pl.when((p != grid.a) & (grid.at(p, q) < chip))
+            def _():
+                first_copy(p, q).wait_send()
+
+    def finish_gchip(c, _):
+        @pl.when(c != chip)
+        def _():
+            gchip_copy(chip, c).wait_send()
+        return 0
+
+    lax.fori_loop(0, nchip, finish_gchip, 0)
+
     @pl.when(core == 0)
     def _():
         pair_copy(chip).wait_recv()
@@ -639,36 +681,10 @@
     router_out[...] = total
 
     gpair_copy(core).wait_send()
-
-    def finish(c, _):
-        @pl.when((c < chip) | ((c == chip) & (core == 1)))
-        def _():
-            pair_copy(c).wait_send()
-
-        @pl.when(c != chip)
-        def _():
-            gchip_copy(chip, c).wait_send()
-        return 0
-
-    lax.fori_loop(0, nchip, finish, 0)
-
-    for q in range(side):
-        for p in range(side):
-            @pl.when((p != grid.a) & (grid.at(p, q) < chip))
-            def _():
-                first_copy(p, q).wait_send()
-
+    for q in range(side):
         @pl.when((q != grid.b) & (grid.at(grid.a, q) < grid.at(last, grid.b)))
         def _():
             second_copy(q).wait_send()
-
-    def finish_tp(t, _):
-        @pl.when(t != mt)
-        def _():
-            tp_copy(mt, t).wait_send()
-        return 0
-
-    lax.fori_loop(0, ntp, finish_tp, 0)
 
 
 def vmem(n=1):
@@ -702,7 +718,7 @@
         compiler_params=pltpu.CompilerParams(
             collective_id=0, has_side_effects=True, vmem_limit_bytes=VMEM_LIMIT),
         name="fetch",
-    )(hidden, queries, keys_values, w_router.reshape(1, width), routed)
+    )(hidden, queries, keys_values, w_router, routed)
 
     live = nseq * cap * LIVE_SHARE[0] // LIVE_SHARE[1]
     span = -(-(live + 15 * nseq) // CHUNK) * CHUNK

time: 77 us -> 73.9 us (0.960)
  Pallas kernels: 72 us -> 70.1 us
  local copies, waits for them, and re-layouts: 4.08 us -> 2.8 us
    pallas_call x1, Pallas kernels: 41.5 us -> 39.4 us  [shards(): pl.pallas_call(functools.partial(return_kernel, nseq, ntp), out_shape=(sh...]
    reshape x1 -> x0, local copies, waits for them, and re-layouts: 1.28 us -> none  [shards(): w_router.reshape(1, width)]
where the time goes in v4:
time: 73.9 us; the launch traced here: 73.6 us
  Pallas kernels  70.1 us (95%)
  local copies, waits for them, and re-layouts  2.8 us (4%)
    pallas_call x1, Pallas kernels, shards(): pl.pallas_call(functools.partial(return_kernel, nseq, ntp), out_shape=(sh...  39.4 us
    pallas_call x1, Pallas kernels, shards(): pl.pallas_call(functools.partial(fetch_kernel, nseq, ntp), out_shape=(sha...  20.4 us
    pallas_call x1, Pallas kernels, shards(): pl.pallas_call(functools.partial(attend_kernel, scale), out_shape=(shape(...  10.3 us
    unnamed x2, local copies, waits for them, and re-layouts  2.8 us

profile of v4, /device:TPU:24, one launch (start us, length us, event | category | flops | bytes accessed | tf_op | source)
XLA Modules:
  0.0 73.6 jit_solution(6061520528757200048)
XLA Ops:
  0.6 20.4 %fetch.1 = (bf16[160,1024]{1,0:T(8,128)(2,1)}, bf16[8,160,128]{2,1,0:T(8,128)(2,1)}, bf16[32,160,256]{2,1,0:T(8,128)(2,1)}, f32[8,256]{1,0:T(8,128)}) custom-call(bf16[1280,1024]{1,0:T(8,128)(2,1)} %hid.1, bf16[1280,1024]{1,0:T(8,128)(2,1)} %qry.1, bf16[2,1280,128]{2,1,0:T(8,128)(2,1)} %kv.1, bf16[1024]{0:T(1024)(128)(2,1)} %w.1, s32[1,160]{1,0:T(1,128)} %routed.1), custom_call_target="tpu_custom_call" | custom-call | tf_op jit(solution)/shard_map/fetch/pallas_call | solution.py:707
  21.1 10.3 %attend.1 = (bf16[160,1024]{1,0:T(8,128)(2,1)}, bf16[160,1024]{1,0:T(8,128)(2,1)}, bf16[2,16,160,256]{3,2,1,0:T(8,128)(2,1)}, f32[160,256]{1,0:T(8,128)}, f32[8,256]{1,0:T(8,128)}) custom-call(s32[32]{0:T(128)} %counts.1, bf16[32,160,256]{2,1,0:T(8,128)(2,1)} %get-tuple-element.15.kv_hbm, bf16[1280,128]{1,0:T(8,128)(2,1)} %bitcast.2, ...), custom_call_target="tpu_custom_call" | custom-call | tf_op jit(solution)/shard_map/attend/pallas_call | solution.py:726
  31.4 39.4 %settle.1 = (bf16[2,160,128]{2,1,0:T(8,128)(2,1)}, f32[8,128]{1,0:T(8,128)}) custom-call(bf16[2,16,160,256]{3,2,1,0:T(8,128)(2,1)} %get-tuple-element.20.contrib, f32[160,256]{1,0:T(8,128)} %get-tuple-element.21.own_hbm, f32[8,256]{1,0:T(8,128)} %get-tuple-element.22.gterm, bf16[160,1024]{1,0:T(8,128)(2,1)} %get-tuple-element.23.x_hbm), custom_call_target="tpu_custom_call" | custom-call | tf_op jit(solution)/shard_map/settle/pallas_call | solution.py:744
  70.8 1.5 %copy.13 = bf16[2,160,128]{2,1,0:T(8,128)(2,1)} copy(bf16[2,160,128]{2,1,0:T(8,128)(2,1)} %get-tuple-element.32) | data formatting | bytes 163840
  72.3 1.3 %copy.14 = f32[1024]{0:T(1024)} copy(f32[1024]{0:T(1024)} %bitcast.3) | data formatting | bytes 8192

commit v5 on v4

--- a/solution.py
+++ b/solution.py
@@ -63,8 +63,6 @@
     load_hid = pltpu.make_async_copy(hid, hid_v, lsem.at[1])
     load_qry = pltpu.make_async_copy(qry, qry_v, lsem.at[2])
     load_kv.start()
-    load_hid.start()
-    load_qry.start()
 
     barrier = pltpu.get_barrier_semaphore()
 
@@ -94,6 +92,8 @@
         [jnp.where(col == lane + 128.0 * j, 1.0, 0.0).astype(BF16) for j in range(tok // 128)], axis=1
     )
     load_kv.wait()
+    load_hid.start()
+    load_qry.start()
     held[:, 0:128] = dot_nn(onehot, kv_v[0]).astype(BF16)
     held[:, 128:256] = dot_nn(onehot, kv_v[1]).astype(BF16)
     keep = pltpu.make_async_copy(held, kvall.at[me], lsem.at[3])
@@ -493,12 +493,16 @@
 
     lax.fori_loop(0, ntp, send_tp, 0)
 
+    side0 = math.isqrt(nchip)
+
     def pair_copy(c):
         return pltpu.make_async_remote_copy(
             src_ref=contrib.at[1 - core, c], dst_ref=pair.at[c], send_sem=psem.at[c], recv_sem=prsem.at[c],
             device_id={"seq": sib}, device_id_type=MESH)
 
-    def send_pair(c, _):
+    def send_pair(i, _):
+        c = jnp.where(core == 0, i % side0 * side0 + i // side0, i)
+
         @pl.when((c < chip) | ((c == chip) & (core == 1)))
         def _():
             pair_copy(c).start()
@@ -564,8 +568,10 @@
     p3 = (r1 - p2.astype(F32)).astype(BF16)
     loads[2].wait()
     xs = x[...]
-    share = (dot_nn(jnp.broadcast_to(p1, (16, cap)), xs) + dot_nn(jnp.broadcast_to(p2, (16, cap)), xs)
-             + dot_nn(jnp.broadcast_to(p3, (16, cap)), xs))
+    rows16 = lax.broadcasted_iota(jnp.int32, (16, cap), 0)
+    parts = jnp.where(rows16 == 0, p1.astype(F32), jnp.where(
+        rows16 == 1, p2.astype(F32), jnp.where(rows16 == 2, p3.astype(F32), 0.0))).astype(BF16)
+    share = jnp.sum(dot_nn(parts, xs), axis=0, keepdims=True)
     for i in range(x.shape[1] // 128):
         gpair[core, i:i + 1, :] = share[0:1, i * 128:(i + 1) * 128]
 

time: 73.9 us -> 73.9 us (level)
    pallas_call x1, Pallas kernels: 10.3 us -> 8.63 us  [shards(): pl.pallas_call(functools.partial(attend_kernel, scale), out_shape=(shape(...]
    pallas_call x1, Pallas kernels: 39.4 us -> 41 us  [shards(): pl.pallas_call(functools.partial(return_kernel, nseq, ntp), out_shape=(sh...]
where the time goes in v5:
time: 73.9 us; the launch traced here: 73.6 us
  Pallas kernels  70.1 us (95%)
  local copies, waits for them, and re-layouts  2.8 us (4%)
    pallas_call x1, Pallas kernels, shards(): pl.pallas_call(functools.partial(return_kernel, nseq, ntp), out_shape=(sh...  41 us
    pallas_call x1, Pallas kernels, shards(): pl.pallas_call(functools.partial(fetch_kernel, nseq, ntp), out_shape=(sha...  20.4 us
    pallas_call x1, Pallas kernels, shards(): pl.pallas_call(functools.partial(attend_kernel, scale), out_shape=(shape(...  8.63 us
    unnamed x2, local copies, waits for them, and re-layouts  2.8 us

profile of v5, /device:TPU:24, one launch (start us, length us, event | category | flops | bytes accessed | tf_op | source)
XLA Modules:
  0.0 73.6 jit_solution(8729919523501716718)
XLA Ops:
  0.6 20.4 %fetch.1 = (bf16[160,1024]{1,0:T(8,128)(2,1)}, bf16[8,160,128]{2,1,0:T(8,128)(2,1)}, bf16[32,160,256]{2,1,0:T(8,128)(2,1)}, f32[8,256]{1,0:T(8,128)}) custom-call(bf16[1280,1024]{1,0:T(8,128)(2,1)} %hid.1, bf16[1280,1024]{1,0:T(8,128)(2,1)} %qry.1, bf16[2,1280,128]{2,1,0:T(8,128)(2,1)} %kv.1, bf16[1024]{0:T(1024)(128)(2,1)} %w.1, s32[1,160]{1,0:T(1,128)} %routed.1), custom_call_target="tpu_custom_call" | custom-call | tf_op jit(solution)/shard_map/fetch/pallas_call | solution.py:713
  21.1 8.6 %attend.1 = (bf16[160,1024]{1,0:T(8,128)(2,1)}, bf16[160,1024]{1,0:T(8,128)(2,1)}, bf16[2,16,160,256]{3,2,1,0:T(8,128)(2,1)}, f32[160,256]{1,0:T(8,128)}, f32[8,256]{1,0:T(8,128)}) custom-call(s32[32]{0:T(128)} %counts.1, bf16[32,160,256]{2,1,0:T(8,128)(2,1)} %get-tuple-element.15.kv_hbm, bf16[1280,128]{1,0:T(8,128)(2,1)} %bitcast.2, ...), custom_call_target="tpu_custom_call" | custom-call | tf_op jit(solution)/shard_map/attend/pallas_call | solution.py:732
  29.7 41.0 %settle.1 = (bf16[2,160,128]{2,1,0:T(8,128)(2,1)}, f32[8,128]{1,0:T(8,128)}) custom-call(bf16[2,16,160,256]{3,2,1,0:T(8,128)(2,1)} %get-tuple-element.20.contrib, f32[160,256]{1,0:T(8,128)} %get-tuple-element.21.own_hbm, f32[8,256]{1,0:T(8,128)} %get-tuple-element.22.gterm, bf16[160,1024]{1,0:T(8,128)(2,1)} %get-tuple-element.23.x_hbm), custom_call_target="tpu_custom_call" | custom-call | tf_op jit(solution)/shard_map/settle/pallas_call | solution.py:750
  70.8 1.5 %copy.13 = bf16[2,160,128]{2,1,0:T(8,128)(2,1)} copy(bf16[2,160,128]{2,1,0:T(8,128)(2,1)} %get-tuple-element.32) | data formatting | bytes 163840
  72.3 1.3 %copy.14 = f32[1024]{0:T(1024)} copy(f32[1024]{0:T(1024)} %bitcast.3) | data formatting | bytes 8192

commit v6 on v4

--- a/solution.py
+++ b/solution.py
@@ -687,6 +687,11 @@
             second_copy(q).wait_send()
 
 
+def hand_kernel(dkv, router, dkv_out, router_out):
+    dkv_out[...] = dkv[...]
+    router_out[...] = router[...]
+
+
 def vmem(n=1):
     specs = [pl.BlockSpec(memory_space=pltpu.VMEM) for _ in range(n)]
     return specs if n > 1 else specs[0]
@@ -759,6 +764,13 @@
             collective_id=1, has_side_effects=True, vmem_limit_bytes=VMEM_LIMIT),
         name="settle",
     )(contrib, own, gterm, x)
+    dkv, router = pl.pallas_call(
+        hand_kernel,
+        out_shape=(shape((2, cap, 128), BF16), shape((width // 128, 128), F32)),
+        in_specs=vmem(2),
+        out_specs=tuple(vmem(2)),
+        name="hand",
+    )(dkv, router)
     return branch, dq, dkv, router.reshape(width)
 
 

time: 73.9 us -> 72.7 us (0.984)
  local copies, waits for them, and re-layouts: 2.8 us -> 0 us
  Pallas kernels: 70.1 us -> 71.9 us
    unnamed x2 -> x0, local copies, waits for them, and re-layouts: 2.8 us -> none
    pallas_call x0 -> x1, Pallas kernels: none -> 1.53 us  [shards(): pl.pallas_call(hand_kernel, out_shape=(shape((2, cap, 128), BF16), shape(...]
where the time goes in v6:
time: 72.7 us; the launch traced here: 72.5 us
  Pallas kernels  71.9 us (99%)
    pallas_call x1, Pallas kernels, shards(): pl.pallas_call(functools.partial(return_kernel, nseq, ntp), out_shape=(sh...  39.6 us
    pallas_call x1, Pallas kernels, shards(): pl.pallas_call(functools.partial(fetch_kernel, nseq, ntp), out_shape=(sha...  20.4 us
    pallas_call x1, Pallas kernels, shards(): pl.pallas_call(functools.partial(attend_kernel, scale), out_shape=(shape(...  10.3 us
    pallas_call x1, Pallas kernels, shards(): pl.pallas_call(hand_kernel, out_shape=(shape((2, cap, 128), BF16), shape(...  1.53 us

profile of v6, /device:TPU:24, one launch (start us, length us, event | category | flops | bytes accessed | tf_op | source)
XLA Modules:
  0.0 72.5 jit_solution(3964632125928192636)
XLA Ops:
  0.6 20.4 %fetch.1 = (bf16[160,1024]{1,0:T(8,128)(2,1)}, bf16[8,160,128]{2,1,0:T(8,128)(2,1)}, bf16[32,160,256]{2,1,0:T(8,128)(2,1)}, f32[8,256]{1,0:T(8,128)}) custom-call(bf16[1280,1024]{1,0:T(8,128)(2,1)} %hid.1, bf16[1280,1024]{1,0:T(8,128)(2,1)} %qry.1, bf16[2,1280,128]{2,1,0:T(8,128)(2,1)} %kv.1, bf16[1024]{0:T(1024)(128)(2,1)} %w.1, s32[1,160]{1,0:T(1,128)} %routed.1), custom_call_target="tpu_custom_call" | custom-call | tf_op jit(solution)/shard_map/fetch/pallas_call | solution.py:712
  21.1 10.3 %attend.1 = (bf16[160,1024]{1,0:T(8,128)(2,1)}, bf16[160,1024]{1,0:T(8,128)(2,1)}, bf16[2,16,160,256]{3,2,1,0:T(8,128)(2,1)}, f32[160,256]{1,0:T(8,128)}, f32[8,256]{1,0:T(8,128)}) custom-call(s32[32]{0:T(128)} %counts.1, bf16[32,160,256]{2,1,0:T(8,128)(2,1)} %get-tuple-element.17.kv_hbm, bf16[1280,128]{1,0:T(8,128)(2,1)} %bitcast.2, ...), custom_call_target="tpu_custom_call" | custom-call | tf_op jit(solution)/shard_map/attend/pallas_call | solution.py:731
  31.4 39.6 %settle.1 = (bf16[2,160,128]{2,1,0:T(8,128)(2,1)}, f32[8,128]{1,0:T(8,128)}) custom-call(bf16[2,16,160,256]{3,2,1,0:T(8,128)(2,1)} %get-tuple-element.22.contrib, f32[160,256]{1,0:T(8,128)} %get-tuple-element.23.own_hbm, f32[8,256]{1,0:T(8,128)} %get-tuple-element.24.gterm, bf16[160,1024]{1,0:T(8,128)(2,1)} %get-tuple-element.25.x_hbm), custom_call_target="tpu_custom_call" | custom-call | tf_op jit(solution)/shard_map/settle/pallas_call | solution.py:749
  71.0 1.5 %hand.1 = (bf16[2,160,128]{2,1,0:T(8,128)(2,1)}, f32[8,128]{1,0:T(8,128)}) custom-call(bf16[2,160,128]{2,1,0:T(8,128)(2,1)} %get-tuple-element.26.dkv, f32[8,128]{1,0:T(8,128)} %get-tuple-element.27.router), custom_call_target="tpu_custom_call" | custom-call | tf_op jit(solution)/shard_map/hand/pallas_call | solution.py:767
